TPU v7x, 128 devices: a whole 4x4x4 slice. The times are simulated.
128 devices in a mesh: sp: 8 (over x, core), ep: 16 (over z, y).
Axes of the slice: x: 4, y: 4, z: 4, core: 2. Of those that a mesh axis runs over, the one named last changes fastest.
Arguments:
- latent: bfloat16 [16, 1024, 4096], P('ep', 'sp'), may hold values from -36 to 36
- attention_in: bfloat16 [16, 1024, 3, 4096], P('ep', 'sp'), may hold values from -6 to 6
- out_weight: bfloat16 [4096, 4096], P('sp'), may hold values from -0.09375 to 0.09375
- modulation: float32 [4, 4096], replicated, may hold values from -4 to 4
- route_experts: int32 [16, 1024, 2], P('ep', 'sp'), may hold values from 0 to 31, as said below
- route_slots: int32 [16, 1024, 2], P('ep', 'sp'), may hold values from 0 to 11, as said below
- route_gates: float32 [16, 1024, 2], P('ep', 'sp'), may hold values from 0.1 to 1
- gate_weight: bfloat16 [16, 4096, 4096], P('ep', None, 'sp'), may hold values from -0.09375 to 0.09375
- up_weight: bfloat16 [16, 4096, 4096], P('ep', None, 'sp'), may hold values from -0.09375 to 0.09375
- down_weight: bfloat16 [16, 4096, 4096], P('ep', 'sp'), may hold values from -0.125 to 0.125
Outputs:
- block_out: bfloat16 [16, 1024, 4096], P('ep', 'sp')
Inputs may be any that keep to these rules, and one draw needn't show every extreme that they name: `route_experts`: each token names two different experts. Among the 128 tokens of one device block no expert is named more than 12 times; in every device block some expert is named exactly 12 times, and one expert is named exactly 12 times in every device block. `route_slots`: the routes of one device block to one expert hold distinct slots.
All inputs are finite; a program needn't handle non-finite values.
Results may differ from a plain program's by a relative error of at most 0.013.
Values may be sent and summed in bfloat16 or wider, within the bound.
A program may use at most 192 MiB of HBM per device.

v0:
```python
import math

import jax
import jax.numpy as jnp
from jax import lax
from jax.sharding import PartitionSpec as P

HD = 128


def attend(block):
    queries = block[:, 0, 0]
    key_rows = block[:, 1, 0]
    value_rows = block[:, 2, 0]
    score_scale = 1.0 / math.sqrt(HD)
    scores = (
        jnp.einsum("qhd,khd->hqk", queries, key_rows, preferred_element_type=jnp.float32)
        * score_scale
    )
    top_rows = jnp.max(scores, axis=-1, keepdims=True)
    lifted = jnp.exp(scores - top_rows)
    weights = (lifted / jnp.sum(lifted, axis=-1, keepdims=True)).astype(jnp.bfloat16)
    mixed = jnp.einsum("hqk,khd->qhd", weights, value_rows, preferred_element_type=jnp.float32)
    return mixed.astype(jnp.bfloat16)


def feed_forward(rows, gate_shard, up_shard, down_shard):
    gate_part = jnp.dot(rows, gate_shard, preferred_element_type=jnp.float32)
    up_part = jnp.dot(rows, up_shard, preferred_element_type=jnp.float32)
    activation = (jax.nn.silu(gate_part) * up_part).astype(jnp.bfloat16)
    return jnp.dot(activation, down_shard, preferred_element_type=jnp.float32).astype(jnp.bfloat16)


def local(
    latent,
    attention_in,
    out_weight,
    modulation,
    route_experts,
    route_slots,
    route_gates,
    gate_weight,
    up_weight,
    down_weight,
):
    n_sp = lax.axis_size("sp")
    n_ep = lax.axis_size("ep")
    tokens = latent.shape[1]
    width = latent.shape[2]
    group_heads = out_weight.shape[0] // HD
    window_len = tokens * n_sp
    packed = attention_in[0].reshape(tokens, 3, n_sp, group_heads, HD)
    attended = attend(lax.all_to_all(packed, "sp", split_axis=2, concat_axis=0, tiled=True))
    flat_heads = attended.reshape(window_len, group_heads * HD)
    projected = lax.psum_scatter(
        jnp.dot(flat_heads, out_weight, preferred_element_type=jnp.float32).astype(jnp.bfloat16),
        "sp",
        scatter_dimension=0,
        tiled=True,
    ).astype(jnp.float32)
    residual = latent[0].astype(jnp.float32) + modulation[0] * projected
    row_mean = jnp.mean(residual, axis=-1, keepdims=True)
    centered = residual - row_mean
    variance = jnp.mean(centered * centered, axis=-1, keepdims=True)
    normed = centered * lax.rsqrt(variance + 1e-06)
    moe_in = (normed * (1.0 + modulation[2]) + modulation[1]).astype(jnp.bfloat16)
    experts_count = 2 * n_ep
    capacity = max(2, 3 * tokens // experts_count)
    shard_count = n_sp // 2
    cell_index = route_experts[0] * capacity + route_slots[0]
    slot_grid = jnp.arange(experts_count * capacity, dtype=jnp.int32)
    one_hot = (
        (cell_index[:, 0:1] == slot_grid[None, :]) | (cell_index[:, 1:2] == slot_grid[None, :])
    ).astype(jnp.bfloat16)
    dispatched = jnp.einsum(
        "tc,td->cd", one_hot, moe_in, preferred_element_type=jnp.float32
    ).astype(jnp.bfloat16)
    by_expert = dispatched.reshape(n_ep, 2, capacity, width)
    spread = jnp.broadcast_to(
        jnp.transpose(by_expert, (1, 0, 2, 3))[:, None], (2, shard_count, n_ep, capacity, width)
    )
    spread = spread.reshape(n_sp * n_ep, capacity, width)
    rows = lax.all_to_all(spread, ("sp", "ep"), split_axis=0, concat_axis=0, tiled=True)
    partial_value = feed_forward(
        rows.reshape(-1, width), gate_weight[0], up_weight[0], down_weight[0]
    ).reshape(rows.shape)
    returned = lax.all_to_all(partial_value, ("sp", "ep"), split_axis=0, concat_axis=0, tiled=True)
    summed = jnp.sum(
        returned.reshape(2, shard_count, n_ep, capacity, width).astype(jnp.float32), axis=1
    )
    per_expert = jnp.transpose(summed, (1, 0, 2, 3)).reshape(experts_count * capacity, width)
    picked = jnp.take(per_expert, cell_index.reshape(-1), axis=0).reshape(tokens, 2, width)
    gate_values = route_gates[0]
    combined = gate_values[:, 0:1] * picked[:, 0] + gate_values[:, 1:2] * picked[:, 1]
    return (residual + modulation[3] * combined).astype(jnp.bfloat16)[None]


def solution(mesh):
    return jax.shard_map(
        local,
        mesh=mesh,
        in_specs=(
            P("ep", "sp", None),
            P("ep", "sp", None, None),
            P("sp", None),
            P(),
            P("ep", "sp", None),
            P("ep", "sp", None),
            P("ep", "sp", None),
            P("ep", None, "sp"),
            P("ep", None, "sp"),
            P("ep", "sp", None),
        ),
        out_specs=P("ep", "sp", None),
        check_vma=False,
    )
```

profile of v0, /device:TPU:14, one launch (start us, length us, event | category | flops | bytes accessed | tf_op | source)
XLA Modules:
  0.0 722.0 jit_solution(17039240418239454661)
XLA Ops:
  6.5 0.0 reduce-scatter.2.cloned.1.call-start
  6.5 4.7 copy.28
  11.2 3.5 copy.29
  14.7 41.4 %all_to_all.28 = bf16[128,3,8,4,128]{4,0,3,1,2:T(8,128)(2,1)S(1)} all-to-all(bf16[128,3,8,4,128]{4,0,3,1,2:T(8,128)(2,1)S(1)} %copy.29), channel_id=1, replica_groups=mesh['sp'=8,'ep'=16] {'sp'}, dimensions={2} | all-to-all | bytes 6291456 | tf_op jit(solution)/shard_map/all_to_all | solution.py:53
  56.1 0.2 copy.30
  56.3 8.1 %fusion.28 = f32[4,1024,1024]{1,2,0:T(8,128)} fusion(bf16[1024,3,1,4,128]{4,0,3,2,1:T(8,128)(2,1)S(1)} %bitcast.95), kind=kOutput, calls=%fused_computation.36 | convolution fusion | flops 1073741824 | bytes 18874368 | tf_op jit(solution)/shard_map/qhd,khd->hqk/dot_general | solution.py:17
  64.4 12.6 %fusion.50 = f32[4,1024]{1,0:T(4,128)S(1)} fusion(f32[4,1024,1024]{1,2,0:T(8,128)} %fusion.28), kind=kOutput, calls=%fused_computation.67 | output fusion | flops 16778240 | bytes 16793600 | tf_op jit(solution)/shard_map/sub | solution.py:21
  77.0 16.4 %fusion.26 = bf16[4,1024,128]{1,2,0:T(8,128)(2,1)} fusion(f32[4,1024]{1,0:T(4,128)S(1)} %fusion.50, bf16[1024,3,1,4,128]{4,0,3,2,1:T(8,128)(2,1)S(1)} %bitcast.96, f32[4,1024,1024]{1,2,0:T(8,128)} %fusion.28), kind=kOutput, calls=%fused_computation.32 | convolution fusion | flops 1095242752 | bytes 35667968 | tf_op jit(solution)/shard_map/hqk,khd->qhd/dot_general | solution.py:23
  93.4 10.4 %convolution_convert_fusion.1 = bf16[1024,4096]{1,0:T(8,128)(2,1)} fusion(bf16[1024,512]{0,1:T(8,128)(2,1)} %bitcast.109, bf16[512,4096]{1,0:T(8,128)(2,1)} %param.12), kind=kOutput, calls=%fused_computation.10 | convolution fusion | flops 4299161600 | bytes 13631488 | tf_op jit(solution)/shard_map/dot_general | solution.py:56
  103.8 0.0 copy-start.5
  103.8 0.0 copy-start.6
  103.8 0.0 copy-start.4
  103.8 0.0 copy-start
  103.8 0.0 reduce-scatter.2.cloned.1.call-update
  103.8 0.6 copy-done.5
  104.5 0.0 copy-done.6
  104.5 0.2 copy-done.4
  104.6 0.1 fusion.49
  104.7 51.8 %reduce-scatter.2.cloned.1.call-done = bf16[128,4096]{1,0:T(8,128)(2,1)} async-done(((bf16[1024,4096]{1,0:T(8,128)(2,1)}), bf16[128,4096]{1,0:T(8,128)(2,1)}) %reduce-scatter.2.cloned.1.call-update) | async-done | bytes 1048592 | tf_op jit(solution)/shard_map/reduce_scatter | solution.py:55
  156.5 0.0 copy-start.2
  156.5 0.0 copy-done
  156.5 1.7 fusion.27
  158.2 1.8 multiply_reduce_fusion.1
  160.0 0.0 copy-done.2
  160.0 2.4 convolution_convert_fusion.2
  162.4 2.8 reshape.93
  165.2 2.5 copy.33
  167.7 2.2 broadcast_in_dim.12
  169.8 196.3 %all_to_all.29 = bf16[128,12,4096]{2,1,0:T(8,128)(2,1)} all-to-all(bf16[128,12,4096]{2,1,0:T(8,128)(2,1)S(1)} %bitcast.92), channel_id=1, replica_groups=mesh['sp'=8,'ep'=16] {'sp','ep'}, dimensions={0} | all-to-all | bytes 25165824 | tf_op jit(solution)/shard_map/all_to_all | solution.py:83
  366.2 18.1 %reshape.95 = bf16[1536,4096]{1,0:T(8,128)(2,1)} reshape(bf16[128,12,4096]{2,1,0:T(8,128)(2,1)} %all_to_all.29) | data formatting | bytes 25165824 | tf_op jit(solution)/shard_map/reshape | solution.py:85
  384.3 10.5 %fusion.9 = f32[1536,512]{1,0:T(8,128)S(1)} fusion(bf16[1536,4096]{1,0:T(8,128)(2,1)} %reshape.95, bf16[1,4096,512]{2,1,0:T(8,128)(2,1)} %param.17), kind=kOutput, calls=%fused_computation.15 | convolution fusion | flops 6442450944 | bytes 19922944 | tf_op jit(solution)/shard_map/dot_general | solution.py:28
  394.7 21.5 %convolution_convert_fusion = bf16[1536,4096]{1,0:T(8,128)(2,1)} fusion(bf16[1,512,4096]{2,1,0:T(8,128)(2,1)} %param.19, bf16[1536,4096]{1,0:T(8,128)(2,1)} %reshape.95, bf16[1,4096,512]{2,1,0:T(8,128)(2,1)} %param.18, f32[1536,512]{1,0:T(8,128)S(1)} %fusion.9), kind=kOutput, calls=%fused_computation.5 | convolution fusion | flops 12895911936 | bytes 36700160 | tf_op jit(solution)/shard_map/dot_general | solution.py:31
  416.2 17.9 %reshape.96 = bf16[128,12,4096]{2,1,0:T(8,128)(2,1)} reshape(bf16[1536,4096]{1,0:T(8,128)(2,1)} %convolution_convert_fusion) | data formatting | bytes 25165824 | tf_op jit(solution)/shard_map/reshape | solution.py:86
  434.1 0.0 copy-start.7
  434.1 14.1 %all-to-all-start.2 = ((bf16[128,12,4096]{2,1,0:T(8,128)(2,1)}), bf16[128,12,4096]{2,1,0:T(8,128)(2,1)}, u32[]{:S(2)}, u32[]{:S(2)}) async-start(bf16[128,12,4096]{2,1,0:T(8,128)(2,1)} %reshape.96), calls=%async_computation.3 | async-start | bytes 33554432 | tf_op jit(solution)/shard_map/all_to_all | solution.py:87
  448.2 0.1 copy.35
  448.3 0.1 add.98
  448.5 0.0 copy-done.7
  448.5 224.2 %all-to-all-done.2 = bf16[128,12,4096]{2,1,0:T(8,128)(2,1)} async-done(((bf16[128,12,4096]{2,1,0:T(8,128)(2,1)}), bf16[128,12,4096]{2,1,0:T(8,128)(2,1)}, u32[]{:S(2)}, u32[]{:S(2)}) %all-to-all-start.2) | async-done | bytes 12582944 | tf_op jit(solution)/shard_map/all_to_all | solution.py:87
  672.7 9.8 %convert_reduce_fusion = f32[2,16,12,4096]{3,2,1,0:T(8,128)S(1)} fusion(bf16[2,4,16,12,4096]{4,3,2,1,0:T(8,128)(2,1)} %bitcast.34), kind=kLoop, calls=%fused_computation.2 | loop fusion | flops 11010048 | bytes 18874368 | tf_op jit(solution)/shard_map/reduce_sum | solution.py:88
  682.5 3.9 copy.34
  686.3 7.7 %reshape.97 = f32[384,4096]{1,0:T(8,128)} reshape(f32[16,2,12,4096]{3,2,1,0:T(8,128)} %copy.34) | data formatting | bytes 12582912 | tf_op jit(solution)/shard_map/reshape | solution.py:91
  694.0 8.6 %gather_fusion = f32[256,4096]{1,0:T(8,128)} fusion(f32[384,4096]{1,0:T(8,128)} %reshape.97, s32[1024]{0:T(1024)S(1)} %pad_clamp_fusion), kind=kCustom, calls=%fused_computation | custom fusion | bytes 8389632 | tf_op jit(solution)/shard_map/jit(_take)/gather | solution.py:92
  702.6 5.8 gather.7
  708.4 5.0 copy_select_fusion
  713.5 0.0 copy-done.1
  713.5 0.0 copy-done.3
  713.5 1.7 fusion.35
  (9 shorter events, 0.0 us)
Async XLA Ops:
  6.5 149.9 %reduce-scatter.2.cloned.1.call-start = ((), (), s32[]{:S(2)}) async-start(), calls=%async_computation.4 | async-start | bytes 9437184 | tf_op jit(solution)/shard_map/reduce_scatter | solution.py:55
  103.8 0.7 copy-start.5
  103.8 0.7 copy-start.6
  103.8 0.9 copy-start.4
  103.8 52.7 %copy-start = (bf16[1,128,4096]{2,1,0:T(8,128)(2,1)S(1)}, bf16[1,128,4096]{2,1,0:T(8,128)(2,1)}, u32[]{:S(2)}) copy-start(bf16[1,128,4096]{2,1,0:T(8,128)(2,1)} %param.10) | copy-start | bytes 3145732
  156.5 3.5 copy-start.2
  434.1 14.4 %copy-start.7 = (f32[1,128,2]{1,2,0:T(2,128)S(1)}, f32[1,128,2]{1,2,0:T(2,128)}, u32[]{:S(2)}) copy-start(f32[1,128,2]{1,2,0:T(2,128)} %param.16) | copy-start | bytes 3076
  434.1 238.6 %all-to-all-start.2 = ((bf16[128,12,4096]{2,1,0:T(8,128)(2,1)}), bf16[128,12,4096]{2,1,0:T(8,128)(2,1)}, u32[]{:S(2)}, u32[]{:S(2)}) async-start(bf16[128,12,4096]{2,1,0:T(8,128)(2,1)} %reshape.96), calls=%async_computation.3 | async-start | bytes 33554432 | tf_op jit(solution)/shard_map/all_to_all | solution.py:87
  708.4 5.1 copy-start.1
  708.4 5.1 copy-start.3
Sparse Core Ops, SparseCore 0:
  103.9 52.4 reduce-scatter.1
where the time goes:
time: 724 us; the launch traced here: 722 us
  waiting for transfers between devices  276 us (38%)
  blocking collectives  238 us (33%)
  local copies, waits for them, and re-layouts  78.8 us (11%)
  matrix products  69.2 us (10%)
  other arithmetic  32.7 us (5%)
  starting transfers between devices  14.1 us (2%)
  between operations  13.5 us (2%)
    all_to_all x1, waiting for transfers between devices, local(): lax.all_to_all(partial_value, ('sp', 'ep'), split_axis=0, concat_axis=0,...  224 us
    all_to_all x1, blocking collectives, local(): lax.all_to_all(spread, ('sp', 'ep'), split_axis=0, concat_axis=0, tiled=T...  196 us
    reduce_scatter x1, waiting for transfers between devices, local(): lax.psum_scatter(jnp.dot(flat_heads, out_weight, preferred_element_type=j...  51.8 us
    all_to_all x1, blocking collectives, local(): lax.all_to_all(packed, 'sp', split_axis=2, concat_axis=0, tiled=True)  41.4 us
    dot_general x1, matrix products, feed_forward(): jnp.dot(activation, down_shard, preferred_element_type=jnp.float32)  21.5 us
    reshape x1, local copies, waits for them, and re-layouts, local(): rows.reshape(-1, width)  18.1 us
    reshape x1, local copies, waits for them, and re-layouts, local(): partial_value = feed_forward(rows.reshape(-1, width), gate_weight[0], up_...  17.9 us
    dot_general x1, matrix products, attend(): jnp.einsum('hqk,khd->qhd', weights, value_rows, preferred_element_type=jn...  16.4 us
  transfers between devices with their start and end apart: 2, of which 2 were waited for; matrix products, arithmetic and copies ran while one was open for 0% of the time, Pallas kernels for 0%

commit v1 on v0

v1 whole, which is shorter than its diff:
```python
import functools
import math

import jax
import jax.numpy as jnp
from jax import lax
from jax.experimental import pallas as pl
from jax.experimental.pallas import tpu as pltpu
from jax.sharding import PartitionSpec as P

HD = 128
MESH = pl.DeviceIdType.MESH

PLANE = (
    (1, 0), (0, 1), (3, 0), (0, 3), (1, 1), (3, 3), (2, 0), (0, 2),
    (1, 3), (3, 1), (2, 1), (1, 2), (2, 3), (3, 2), (2, 2),
)
LINE = (1, 3, 2)
CAP = 12
BLOCK_SLOTS = 4 * CAP
LAG = 2
W_SLOTS = 3


def attend(block):
    queries = block[:, 0, 0]
    key_rows = block[:, 1, 0]
    value_rows = block[:, 2, 0]
    score_scale = 1.0 / math.sqrt(HD)
    scores = (
        jnp.einsum("qhd,khd->hqk", queries, key_rows, preferred_element_type=jnp.float32)
        * score_scale
    )
    top_rows = jnp.max(scores, axis=-1, keepdims=True)
    lifted = jnp.exp(scores - top_rows)
    weights = (lifted / jnp.sum(lifted, axis=-1, keepdims=True)).astype(jnp.bfloat16)
    mixed = jnp.einsum("hqk,khd->qhd", weights, value_rows, preferred_element_type=jnp.float32)
    return mixed.astype(jnp.bfloat16)


def expert_kernel(
    chunks,
    moe_ref, res_ref, gate_ref, packs_ref, wg_own, wg_far, wu_own, wu_far, wd_own, wd_far,
    out_ref,
    tok, send, recv, back, sums, acc_g, acc_u, act, wg, wu, wd, spread, merge, own,
    ag_s, ag_r, d_s, d_r, r_s, r_r, x_s, x_r, w_sem, wd_sem,
):
    sp, ep = lax.axis_index("sp"), lax.axis_index("ep")
    x, core = sp // 2, sp % 2
    z, y = ep // 4, ep % 4
    F = tok.shape[3]
    half = wg_own.shape[1]
    n_rows = send.shape[1]
    n_tok = 4 * tok.shape[2]
    tile = 256

    def x_peer(d):
        return (x + d) % 4

    def x_dev(d):
        return (x_peer(d) * 2 + core, ep)

    def plane_peer(o):
        return ((z + o[0]) % 4) * 4 + (y + o[1]) % 4

    barrier = pltpu.get_barrier_semaphore()
    for d in LINE:
        pl.semaphore_signal(barrier, inc=1, device_id=x_dev(d), device_id_type=MESH)
    for o in PLANE:
        pl.semaphore_signal(barrier, inc=1, device_id=(sp, plane_peer(o)), device_id_type=MESH)

    def cols(c):
        return pl.ds(pl.multiple_of(c * F, F), F)

    def seat(p):
        return pl.ds(pl.multiple_of(p * BLOCK_SLOTS, 16), BLOCK_SLOTS)

    def w_copies(k):
        s = k % W_SLOTS
        out = []
        for i, (src, dst, at) in enumerate(
            ((wg_own, wg, 0), (wg_far, wg, half), (wu_own, wu, 0), (wu_far, wu, half))
        ):
            out.append(
                pltpu.make_async_copy(src.at[cols(k), :], dst.at[s, :, pl.ds(at, half)], w_sem.at[s, i])
            )
        return out

    def wd_copies(k):
        s = k % W_SLOTS
        return [
            pltpu.make_async_copy(src.at[:, cols(k)], wd.at[s, pl.ds(at, half), :], wd_sem.at[s, i])
            for i, (src, at) in enumerate(((wd_own, 0), (wd_far, half)))
        ]

    def ag_copy(c, i):
        return pltpu.make_async_remote_copy(
            moe_ref.at[:, cols(c)], tok.at[c, x], ag_s.at[c, i], ag_r.at[c, i],
            device_id=x_dev(LINE[i]), device_id_type=MESH,
        )

    def plane_copy(c, i, dst, s_sem, r_sem):
        peer = plane_peer(PLANE[i])
        return pltpu.make_async_remote_copy(
            send.at[c, seat(peer)], dst.at[c, seat(ep)], s_sem.at[c, i], r_sem.at[c, i],
            device_id=(sp, peer), device_id_type=MESH,
        )

    def sum_copy(c, i):
        return pltpu.make_async_remote_copy(
            tok.at[c, x_peer(LINE[i])], sums.at[c, i], x_s.at[c, i], x_r.at[c, i],
            device_id=x_dev(LINE[i]), device_id_type=MESH,
        )

    for k in range(W_SLOTS):
        for cp in w_copies(k) + wd_copies(k):
            cp.start()

    pl.semaphore_wait(barrier, len(LINE) + len(PLANE))

    @pl.loop(0, chunks)
    def _(c):
        for i in range(3):
            ag_copy(c, i).start()

    row = lax.broadcasted_iota(jnp.int32, (n_rows, 1), 0)
    pair, rest = row // BLOCK_SLOTS, row % BLOCK_SLOTS
    block, slot = rest // CAP, rest % CAP
    wanted = (2 * pair + x // 2) * CAP + slot
    for b in range(4):
        at = slice(b * 128, (b + 1) * 128)
        key = jnp.where(block == b, wanted, -1).astype(jnp.float32)
        first = packs_ref[b, 0:1, :] == key
        second = packs_ref[b, 1:2, :] == key
        spread[:, at] = jnp.where(first | second, 1.0, 0.0).astype(jnp.bfloat16)
        weight = jnp.where(first, packs_ref[b, 2:3, :], 0.0) + jnp.where(second, packs_ref[b, 3:4, :], 0.0)
        merge[at, :] = weight.T.astype(jnp.bfloat16)

    acc_g[...] = jnp.zeros_like(acc_g)
    acc_u[...] = jnp.zeros_like(acc_u)

    @pl.loop(0, chunks + LAG)
    def _(step):
        @pl.when(step < chunks)
        def _():
            c = step
            tok[c, x] = moe_ref[:, cols(c)]
            for i in range(3):
                ag_copy(c, i).wait_recv()
            lines = tok[c].reshape(n_tok, F)

            @pl.loop(0, n_rows // tile)
            def _(m):
                at = pl.ds(pl.multiple_of(m * tile, tile), tile)
                send[c, at, :] = jnp.dot(
                    spread[at, :], lines, preferred_element_type=jnp.float32
                ).astype(jnp.bfloat16)

            for i in range(len(PLANE)):
                plane_copy(c, i, recv, d_s, d_r).start()
            recv[c, seat(ep), :] = send[c, seat(ep), :]

        @pl.when(step >= LAG)
        def _():
            k = step - LAG
            s = k % W_SLOTS
            for cp in w_copies(k):
                cp.wait()
            for i in range(len(PLANE)):
                plane_copy(k, i, recv, d_s, d_r).wait_recv()

            @pl.loop(0, n_rows // tile)
            def _(m):
                at = pl.ds(pl.multiple_of(m * tile, tile), tile)
                lines = recv[k, at, :]
                acc_g[at, :] += jnp.dot(lines, wg[s], preferred_element_type=jnp.float32)
                acc_u[at, :] += jnp.dot(lines, wu[s], preferred_element_type=jnp.float32)

            @pl.when(k + W_SLOTS < chunks)
            def _():
                for cp in w_copies(k + W_SLOTS):
                    cp.start()

    @pl.loop(0, n_rows // 64)
    def _(m):
        at = pl.ds(pl.multiple_of(m * 64, 64), 64)
        g = acc_g[at, :]
        act[at, :] = (g / (1.0 + jnp.exp(-g)) * acc_u[at, :]).astype(jnp.bfloat16)

    @pl.loop(0, chunks + 2 * LAG)
    def _(step):
        @pl.when(step < chunks)
        def _():
            c = step
            s = c % W_SLOTS
            for cp in wd_copies(c):
                cp.wait()
            for i in range(len(PLANE)):
                plane_copy(c, i, recv, d_s, d_r).wait_send()

            @pl.loop(0, n_rows // tile)
            def _(m):
                at = pl.ds(pl.multiple_of(m * tile, tile), tile)
                send[c, at, :] = jnp.dot(
                    act[at, :], wd[s], preferred_element_type=jnp.float32
                ).astype(jnp.bfloat16)

            for i in range(len(PLANE)):
                plane_copy(c, i, back, r_s, r_r).start()
            back[c, seat(ep), :] = send[c, seat(ep), :]

            @pl.when(c + W_SLOTS < chunks)
            def _():
                for cp in wd_copies(c + W_SLOTS):
                    cp.start()

        @pl.when((step >= LAG) & (step < chunks + LAG))
        def _():
            k = step - LAG
            for i in range(len(PLANE)):
                plane_copy(k, i, back, r_s, r_r).wait_recv()
            lines = back[k]

            @pl.loop(0, 4)
            def _(b):
                at = pl.ds(pl.multiple_of(b * 128, 128), 128)
                part = jnp.dot(merge[at, :], lines, preferred_element_type=jnp.float32)
                tok[k, b] = part.astype(jnp.bfloat16)

                @pl.when(b == x)
                def _():
                    own[k] = part

            for i in range(3):
                sum_copy(k, i).start()

        @pl.when(step >= 2 * LAG)
        def _():
            k = step - 2 * LAG
            total = own[k]
            for i in range(3):
                sum_copy(k, i).wait_recv()
                total = total + sums[k, i].astype(jnp.float32)
            out_ref[:, cols(k)] = (res_ref[:, cols(k)] + gate_ref[:, cols(k)] * total).astype(out_ref.dtype)

    @pl.loop(0, chunks)
    def _(c):
        for i in range(3):
            ag_copy(c, i).wait_send()
            sum_copy(c, i).wait_send()
        for i in range(len(PLANE)):
            plane_copy(c, i, back, r_s, r_r).wait_send()


def experts(moe_in, residual, gate_row, packs, weights):
    tokens, width = moe_in.shape
    n_ep = 16
    chunks = 8
    F = width // chunks
    rows = n_ep * BLOCK_SLOTS
    hidden = 2 * weights[0].shape[1]
    bf, f32 = jnp.bfloat16, jnp.float32
    n_plane = len(PLANE)
    dma = pltpu.SemaphoreType.DMA
    vmem = pl.BlockSpec(memory_space=pltpu.VMEM)
    hbm = pl.BlockSpec(memory_space=pl.ANY)
    return pl.pallas_call(
        functools.partial(expert_kernel, chunks),
        out_shape=jax.ShapeDtypeStruct((tokens, width), bf),
        in_specs=[vmem] * 4 + [hbm] * 6,
        out_specs=vmem,
        scratch_shapes=[
            pltpu.VMEM((chunks, 4, tokens, F), bf),
            pltpu.VMEM((chunks, rows, F), bf),
            pltpu.VMEM((chunks, rows, F), bf),
            pltpu.VMEM((chunks, rows, F), bf),
            pltpu.VMEM((chunks, 3, tokens, F), bf),
            pltpu.VMEM((rows, hidden), f32),
            pltpu.VMEM((rows, hidden), f32),
            pltpu.VMEM((rows, hidden), bf),
            pltpu.VMEM((W_SLOTS, F, hidden), bf),
            pltpu.VMEM((W_SLOTS, F, hidden), bf),
            pltpu.VMEM((W_SLOTS, hidden, F), bf),
            pltpu.VMEM((rows, 4 * tokens), bf),
            pltpu.VMEM((4 * tokens, rows), bf),
            pltpu.VMEM((chunks, tokens, F), f32),
            dma((chunks, 3)), dma((chunks, 3)),
            dma((chunks, n_plane)), dma((chunks, n_plane)),
            dma((chunks, n_plane)), dma((chunks, n_plane)),
            dma((chunks, 3)), dma((chunks, 3)),
            dma((W_SLOTS, 4)), dma((W_SLOTS, 2)),
        ],
        compiler_params=pltpu.CompilerParams(
            collective_id=0, has_side_effects=True, vmem_limit_bytes=62 * 1024 * 1024
        ),
        cost_estimate=pl.CostEstimate(flops=26_000_000_000, bytes_accessed=40_000_000, transcendentals=800_000),
        name="experts",
    )(moe_in, residual, gate_row, packs, *weights)


def local(
    latent,
    attention_in,
    out_weight,
    modulation,
    route_experts,
    route_slots,
    route_gates,
    gate_weight,
    up_weight,
    down_weight,
):
    n_sp = lax.axis_size("sp")
    tokens = latent.shape[1]
    group_heads = out_weight.shape[0] // HD
    window_len = tokens * n_sp
    core = lax.axis_index("sp") % 2

    swap = [(i, i ^ 1) for i in range(n_sp)]
    weights = []
    for w in (gate_weight[0], up_weight[0], down_weight[0]):
        weights += [w, lax.ppermute(w, "sp", swap)]

    cells = (route_experts[0] * CAP + route_slots[0]).astype(jnp.float32)
    pack = jnp.concatenate([cells, route_gates[0], jnp.zeros((tokens, 4), jnp.float32)], axis=1).T
    packs = lax.all_gather(pack, "sp").reshape(n_sp // 2, 2, 8, tokens)
    packs = lax.dynamic_index_in_dim(packs, core, 1, keepdims=False)

    packed = attention_in[0].reshape(tokens, 3, n_sp, group_heads, HD)
    attended = attend(lax.all_to_all(packed, "sp", split_axis=2, concat_axis=0, tiled=True))
    flat_heads = attended.reshape(window_len, group_heads * HD)
    projected = lax.psum_scatter(
        jnp.dot(flat_heads, out_weight, preferred_element_type=jnp.float32).astype(jnp.bfloat16),
        "sp",
        scatter_dimension=0,
        tiled=True,
    ).astype(jnp.float32)
    residual = latent[0].astype(jnp.float32) + modulation[0] * projected
    row_mean = jnp.mean(residual, axis=-1, keepdims=True)
    centered = residual - row_mean
    variance = jnp.mean(centered * centered, axis=-1, keepdims=True)
    normed = centered * lax.rsqrt(variance + 1e-06)
    moe_in = (normed * (1.0 + modulation[2]) + modulation[1]).astype(jnp.bfloat16)
    return experts(moe_in, residual, modulation[3:4], packs, weights)[None]


def solution(mesh):
    return jax.shard_map(
        local,
        mesh=mesh,
        in_specs=(
            P("ep", "sp", None),
            P("ep", "sp", None, None),
            P("sp", None),
            P(),
            P("ep", "sp", None),
            P("ep", "sp", None),
            P("ep", "sp", None),
            P("ep", None, "sp"),
            P("ep", None, "sp"),
            P("ep", "sp", None),
        ),
        out_specs=P("ep", "sp", None),
        check_vma=False,
    )
```

time: 724 us -> 356 us (0.49)
  the two profiles are of different devices: /device:TPU:14 before, /device:TPU:1 now
where the time goes in v1:
time: 356 us; the launch traced here: 350 us
  Pallas kernels  178 us (50%)
  blocking collectives  63.4 us (18%)
  matrix products  34.8 us (10%)
  waiting for transfers between devices  30.1 us (8%)
  other arithmetic  16.7 us (5%)
  between operations  13.5 us (4%)
  local copies, waits for them, and re-layouts  12.4 us (3%)
    pallas_call x1, Pallas kernels, experts(): pl.pallas_call(functools.partial(expert_kernel, chunks), out_shape=jax.Sh...  178 us
    all_to_all x1, blocking collectives, local(): lax.all_to_all(packed, 'sp', split_axis=2, concat_axis=0, tiled=True)  43.5 us
    reduce_scatter x1, waiting for transfers between devices, local(): lax.psum_scatter(jnp.dot(flat_heads, out_weight, preferred_element_type=j...  30 us
    all_gather x1, blocking collectives, local(): packs = lax.all_gather(pack, 'sp').reshape(n_sp // 2, 2, 8, tokens)  19.9 us
    dot_general x1, matrix products, attend(): jnp.einsum('hqk,khd->qhd', weights, value_rows, preferred_element_type=jn...  16.4 us
    sub x1, other arithmetic, attend(): lifted = jnp.exp(scores - top_rows)  12.6 us
    dot_general x1, matrix products, local(): jnp.dot(flat_heads, out_weight, preferred_element_type=jnp.float32)  10.3 us
    dot_general x1, matrix products, attend(): jnp.einsum('qhd,khd->hqk', queries, key_rows, preferred_element_type=jnp....  8.06 us
  transfers between devices with their start and end apart: 4, of which 1 were waited for; matrix products, arithmetic and copies ran while one was open for 1% of the time, Pallas kernels for 0%

profile of v1, /device:TPU:1, one launch (start us, length us, event | category | flops | bytes accessed | tf_op | source)
XLA Modules:
  0.0 350.1 jit_solution(12315005927550013229)
XLA Ops:
  6.5 0.0 reduce-scatter.2.cloned.1.call-start
  6.5 4.7 %copy.22 = bf16[1,128,3,4096]{1,3,2,0:T(8,128)(2,1)} copy(bf16[1,128,3,4096]{3,1,2,0:T(8,128)(2,1)} %param.11) | data formatting | bytes 6291456 | tf_op args[1]
  11.2 3.5 copy.23
  14.7 43.5 %all_to_all.18 = bf16[128,3,8,4,128]{4,0,3,1,2:T(8,128)(2,1)S(1)} all-to-all(bf16[128,3,8,4,128]{4,0,3,1,2:T(8,128)(2,1)S(1)} %copy.23), channel_id=1, replica_groups=mesh['sp'=8,'ep'=16] {'sp'}, dimensions={2} | all-to-all | bytes 6291456 | tf_op jit(solution)/shard_map/all_to_all | solution.py:330
  58.2 0.2 copy.24
  58.4 8.1 %fusion.7 = f32[4,1024,1024]{1,2,0:T(8,128)} fusion(bf16[1024,3,1,4,128]{4,0,3,2,1:T(8,128)(2,1)S(1)} %bitcast.38), kind=kOutput, calls=%fused_computation.14 | convolution fusion | flops 1073741824 | bytes 18874368 | tf_op jit(solution)/shard_map/qhd,khd->hqk/dot_general | solution.py:31
  66.5 12.6 %fusion.18 = f32[4,1024]{1,0:T(4,128)S(1)} fusion(f32[4,1024,1024]{1,2,0:T(8,128)} %fusion.7), kind=kOutput, calls=%fused_computation.27 | output fusion | flops 16778240 | bytes 16793600 | tf_op jit(solution)/shard_map/sub | solution.py:35
  79.1 16.4 %fusion.6 = bf16[4,1024,128]{1,2,0:T(8,128)(2,1)} fusion(f32[4,1024]{1,0:T(4,128)S(1)} %fusion.18, bf16[1024,3,1,4,128]{4,0,3,2,1:T(8,128)(2,1)S(1)} %bitcast.39, f32[4,1024,1024]{1,2,0:T(8,128)} %fusion.7), kind=kOutput, calls=%fused_computation.11 | convolution fusion | flops 1095242752 | bytes 35667968 | tf_op jit(solution)/shard_map/hqk,khd->qhd/dot_general | solution.py:37
  95.5 10.3 %convolution_convert_fusion = bf16[1024,4096]{1,0:T(8,128)(2,1)} fusion(bf16[1024,512]{0,1:T(8,128)(2,1)} %bitcast.54, bf16[512,4096]{1,0:T(8,128)(2,1)} %param.12), kind=kOutput, calls=%fused_computation.7 | convolution fusion | flops 4299161600 | bytes 13631488 | tf_op jit(solution)/shard_map/dot_general | solution.py:333
  105.8 0.0 copy-start.3
  105.8 0.0 copy-start.4
  105.8 0.0 copy-start.5
  105.8 0.0 copy-start.2
  105.8 0.0 copy-start.1
  105.8 0.0 reduce-scatter.2.cloned.1.call-update
  105.8 1.1 collective-permute-start
  107.0 0.3 collective-permute-start.1
  107.2 0.2 collective-permute-start.2
  107.5 0.1 pad.2.clone
  107.5 0.0 copy-done.3
  107.6 0.0 copy-done.4
  107.6 0.0 copy-done.5
  107.6 0.1 maximum_bitcast_fusion
  107.6 19.9 %all-gather = f32[64,128]{1,0:T(8,128)S(1)} all-gather(f32[8,128]{1,0:T(8,128)S(1)} %maximum_bitcast_fusion), channel_id=2, replica_groups=mesh['sp'=8,'ep'=16] {'sp'}, dimensions={0}, use_global_device_ids=true | all-gather | bytes 36864 | tf_op jit(solution)/shard_map/all_gather | solution.py:326
  127.6 0.6 dynamic-slice_bitcast_fusion.packs_ref
  128.2 0.0 copy-done.2
  128.2 0.6 fusion.17
  128.8 30.0 %reduce-scatter.2.cloned.1.call-done = bf16[128,4096]{1,0:T(8,128)(2,1)} async-done(((bf16[1024,4096]{1,0:T(8,128)(2,1)}), bf16[128,4096]{1,0:T(8,128)(2,1)}) %reduce-scatter.2.cloned.1.call-update) | async-done | bytes 1048592 | tf_op jit(solution)/shard_map/reduce_scatter | solution.py:332
  158.9 0.0 copy-done.1
  158.9 1.7 fusion.16
  160.5 0.0 copy-start
  160.6 0.4 multiply_reduce_fusion.1
  160.9 1.0 copy-done
  161.9 1.4 add_convert_fusion.moe_ref
  163.3 0.0 collective-permute-done.wg_far
  163.3 0.0 collective-permute-done.1.wu_far
  163.3 0.0 collective-permute-done.2.wd_far
  163.3 177.7 %experts.1 = bf16[128,4096]{1,0:T(8,128)(2,1)} custom-call(bf16[128,4096]{1,0:T(8,128)(2,1)} %add_convert_fusion.moe_ref, f32[128,4096]{1,0:T(8,128)} %copy-done, f32[1,4096]{1,0:T(1,128)} %get-tuple-element.7.gate_ref, f32[4,8,128]{2,1,0:T(8,128)} %dynamic-slice_bitcast_fusion.packs_ref, bf16[4096,512]{1,0:T(8,128)(2,1)} %bitcast.49, ...), custom_call_target="tpu_custom_call" | custom-call | flops 25999998976 | bytes 40000000 | tf_op jit(solution)/shard_map/experts/pallas_call | solution.py:267
  341.0 2.3 copy.30
  (4 shorter events, 0.0 us)
Async XLA Ops:
  6.5 152.3 %reduce-scatter.2.cloned.1.call-start = ((), (), s32[]{:S(2)}) async-start(), calls=%async_computation.2 | async-start | bytes 9437184 | tf_op jit(solution)/shard_map/reduce_scatter | solution.py:332
  105.8 1.8 copy-start.3
  105.8 1.8 copy-start.4
  105.8 1.8 copy-start.5
  105.8 22.4 %copy-start.2 = (f32[4,4096]{1,0:T(4,128)S(1)}, f32[4,4096]{1,0:T(4,128)}, u32[]{:S(2)}) copy-start(f32[4,4096]{1,0:T(4,128)} %param.13) | copy-start | bytes 196612
  105.8 53.1 %copy-start.1 = (bf16[1,128,4096]{2,1,0:T(8,128)(2,1)S(1)}, bf16[1,128,4096]{2,1,0:T(8,128)(2,1)}, u32[]{:S(2)}) copy-start(bf16[1,128,4096]{2,1,0:T(8,128)(2,1)} %param.10) | copy-start | bytes 3145732
  105.8 57.4 %collective-permute-start = (bf16[4096,512]{1,0:T(8,128)(2,1)}, bf16[4096,512]{1,0:T(8,128)(2,1)}, u32[]{:S(2)}, u32[]{:S(2)}) collective-permute-start(bf16[4096,512]{1,0:T(8,128)(2,1)} %bitcast.48), channel_id=1, source_target_pairs={{0,16},{16,0},{32,48},{48,32},{64,80},{80,64},{96,112},{112,96},{1... | collective-permute-start | bytes 12582920 | tf_op jit(solution)/shard_map/ppermute | solution.py:322
  107.0 56.3 %collective-permute-start.1 = (bf16[4096,512]{1,0:T(8,128)(2,1)}, bf16[4096,512]{1,0:T(8,128)(2,1)}, u32[]{:S(2)}, u32[]{:S(2)}) collective-permute-start(bf16[4096,512]{1,0:T(8,128)(2,1)} %bitcast.50), channel_id=1, source_target_pairs={{0,16},{16,0},{32,48},{48,32},{64,80},{80,64},{96,112},{112,96},{1... | collective-permute-start | bytes 12582920 | tf_op jit(solution)/shard_map/ppermute | solution.py:322
  107.2 56.1 %collective-permute-start.2 = (bf16[512,4096]{1,0:T(8,128)(2,1)}, bf16[512,4096]{1,0:T(8,128)(2,1)}, u32[]{:S(2)}, u32[]{:S(2)}) collective-permute-start(bf16[512,4096]{1,0:T(8,128)(2,1)} %bitcast.52), channel_id=1, source_target_pairs={{0,16},{16,0},{32,48},{48,32},{64,80},{80,64},{96,112},{112,96},{1... | collective-permute-start | bytes 12582920 | tf_op jit(solution)/shard_map/ppermute | solution.py:322
  160.5 1.4 copy-start
Sparse Core Ops, SparseCore 0:
  106.0 52.8 reduce-scatter.1

commit v2 on v1

--- a/solution.py
+++ b/solution.py
@@ -22,20 +22,247 @@
 W_SLOTS = 3
 
 
-def attend(block):
-    queries = block[:, 0, 0]
-    key_rows = block[:, 1, 0]
-    value_rows = block[:, 2, 0]
-    score_scale = 1.0 / math.sqrt(HD)
-    scores = (
-        jnp.einsum("qhd,khd->hqk", queries, key_rows, preferred_element_type=jnp.float32)
-        * score_scale
-    )
-    top_rows = jnp.max(scores, axis=-1, keepdims=True)
-    lifted = jnp.exp(scores - top_rows)
-    weights = (lifted / jnp.sum(lifted, axis=-1, keepdims=True)).astype(jnp.bfloat16)
-    mixed = jnp.einsum("hqk,khd->qhd", weights, value_rows, preferred_element_type=jnp.float32)
-    return mixed.astype(jnp.bfloat16)
+def attention_kernel(
+    chunks,
+    qkv_ref, latent_ref, wo_ref, mod_ref, pack_ref, wg_ref, wu_ref, wd_ref,
+    moe_ref, res_ref, packs_ref, wg_far, wu_far, wd_far,
+    heads, values, att, pair_out, pair_in, turn_out, turn_in, side, side_out, side_in, own,
+    q_s, q_r, q_l, p_s, p_r, t_s, t_r, s_s, s_r, w_s, w_r, k_s, k_r, k_l,
+):
+    sp, ep = lax.axis_index("sp"), lax.axis_index("ep")
+    x, core = sp // 2, sp % 2
+    n_heads, _, window, hd = heads.shape
+    tokens = window // 8
+    F = wo_ref.shape[1] // chunks
+    H = F // 2
+    f32, bf = jnp.float32, jnp.bfloat16
+
+    def x_peer(d):
+        return (x + d) % 4
+
+    def x_dev(d):
+        return (x_peer(d) * 2 + core, ep)
+
+    partner = (x * 2 + 1 - core, ep)
+    others = [(d, k) for d in (2, 1, 3, 0) for k in (0, 1) if (d, k) != (0, 0)]
+
+    def other(i):
+        d, k = others[i]
+        return x_peer(d) * 2 + (core + k) % 2
+
+    def cols(c):
+        return pl.ds(pl.multiple_of(c * F, F), F)
+
+    def block(s):
+        return pl.ds(pl.multiple_of(s * tokens, tokens), tokens)
+
+    def head_cols(s, h):
+        return pl.ds(pl.multiple_of((s * n_heads + h) * hd, hd), hd)
+
+    def head_copy(h, i):
+        to = other(i)
+        return pltpu.make_async_remote_copy(
+            qkv_ref.at[:, :, head_cols(to, h)], heads.at[h, :, block(sp), :], q_s.at[h, i], q_r.at[h, i],
+            device_id=(to, ep), device_id_type=MESH,
+        )
+
+    def head_local(h):
+        return pltpu.make_async_copy(
+            qkv_ref.at[:, :, head_cols(sp, h)], heads.at[h, :, block(sp), :], q_l.at[h]
+        )
+
+    def weight_copy(i):
+        src, dst = ((wg_ref, wg_far), (wu_ref, wu_far), (wd_ref, wd_far))[i]
+        return pltpu.make_async_remote_copy(
+            src, dst, w_s.at[i], w_r.at[i], device_id=partner, device_id_type=MESH
+        )
+
+    def pack_copy(i):
+        return pltpu.make_async_remote_copy(
+            pack_ref, packs_ref.at[x], k_s.at[i], k_r.at[i], device_id=x_dev(LINE[i]), device_id_type=MESH
+        )
+
+    pack_local = pltpu.make_async_copy(pack_ref, packs_ref.at[x], k_l)
+
+    def pair_copy(c):
+        return pltpu.make_async_remote_copy(
+            pair_out.at[c], pair_in.at[c], p_s.at[c], p_r.at[c], device_id=partner, device_id_type=MESH
+        )
+
+    def turn_copy(c, i):
+        return pltpu.make_async_remote_copy(
+            turn_out.at[c, i], turn_in.at[c, i], t_s.at[c, i], t_r.at[c, i],
+            device_id=x_dev((3, 1)[i]), device_id_type=MESH,
+        )
+
+    def side_copy(c, i):
+        return pltpu.make_async_remote_copy(
+            side_out.at[c, i], side_in.at[c, i], s_s.at[c, i], s_r.at[c, i],
+            device_id=x_dev((3, 1)[i]), device_id_type=MESH,
+        )
+
+    barrier = pltpu.get_barrier_semaphore()
+    for i in range(7):
+        pl.semaphore_signal(barrier, inc=1, device_id=(other(i), ep), device_id_type=MESH)
+    pack_local.start()
+    for h in range(n_heads):
+        head_local(h).start()
+    pl.semaphore_wait(barrier, 7)
+
+    @pl.loop(0, n_heads)
+    def _(h):
+        for i in range(7):
+            head_copy(h, i).start()
+
+    for i in range(3):
+        pack_copy(i).start()
+    for i in range(3):
+        weight_copy(i).start()
+
+    values[:, hd:] = jnp.ones((window, hd), bf)
+    factor = math.log2(math.e) / math.sqrt(hd)
+    q_tile = 2 * tokens
+
+    @pl.loop(0, n_heads)
+    def _(h):
+        head_local(h).wait()
+        for i in range(7):
+            head_copy(h, i).wait_recv()
+        values[:, :hd] = heads[h, 2]
+
+        @pl.loop(0, window // q_tile)
+        def _(m):
+            at = pl.ds(pl.multiple_of(m * q_tile, q_tile), q_tile)
+            scores = lax.dot_general(
+                heads[h, 0, at, :], heads[h, 1], (((1,), (1,)), ((), ())), preferred_element_type=f32
+            )
+            top = jnp.max(scores, axis=1, keepdims=True)
+            lifted = jnp.exp2((scores - top) * factor).astype(bf)
+            mixed = jnp.dot(lifted, values[...], preferred_element_type=f32)
+            out = (mixed[:, :hd] / mixed[:, hd:]).astype(bf)
+            to = (block(m), pl.ds(pl.multiple_of(h * hd, hd), hd))
+            att[0, to[0], to[1]] = out[:tokens]
+            att[1, to[0], to[1]] = out[tokens:]
+
+    @pl.loop(0, chunks + 4)
+    def _(step):
+        @pl.when(step < chunks)
+        def _():
+            c = step
+            far = jnp.dot(att[1 - core], wo_ref[:, cols(c)], preferred_element_type=f32)
+            pair_out[c] = far.astype(bf)
+            pair_copy(c).start()
+
+        @pl.when((step >= 1) & (step < chunks + 1))
+        def _():
+            c = step - 1
+            pair_copy(c).wait_recv()
+
+            def part(b):
+                return jnp.dot(
+                    att[core, block(b), :], wo_ref[:, cols(c)], preferred_element_type=f32
+                ) + pair_in[c, block(b), :].astype(f32)
+
+            over = part(x_peer(2)).astype(bf)
+            for i in range(2):
+                turn_out[c, i] = over[:, i * H : (i + 1) * H]
+                turn_copy(c, i).start()
+            side[c, 0] = part(x_peer(3))
+            side[c, 1] = part(x_peer(1))
+            own[c] = part(x)
+
+        @pl.when((step >= 2) & (step < chunks + 2))
+        def _():
+            c = step - 2
+            for i in range(2):
+                turn_copy(c, i).wait_recv()
+                near = slice(i * H, (i + 1) * H)
+                rest = slice((1 - i) * H, (2 - i) * H)
+                side_out[c, i, :, near] = (side[c, i, :, near] + turn_in[c, i].astype(f32)).astype(bf)
+                side_out[c, i, :, rest] = side[c, i, :, rest].astype(bf)
+                side_copy(c, i).start()
+
+        @pl.when(step >= 4)
+        def _():
+            c = step - 4
+            total = own[c]
+            for i in range(2):
+                side_copy(c, i).wait_recv()
+                total = total + side_in[c, i].astype(f32)
+            res_ref[:, cols(c)] = latent_ref[:, cols(c)].astype(f32) + mod_ref[0:1, cols(c)] * total
+
+    @pl.loop(0, tokens // 16)
+    def _(m):
+        at = pl.ds(pl.multiple_of(m * 16, 16), 16)
+        rows = res_ref[at, :]
+        centered = rows - jnp.mean(rows, axis=1, keepdims=True)
+        variance = jnp.mean(centered * centered, axis=1, keepdims=True)
+        normed = centered * lax.rsqrt(variance + 1e-06)
+        moe_ref[at, :] = (normed * (1.0 + mod_ref[2:3, :]) + mod_ref[1:2, :]).astype(bf)
+
+    pack_local.wait()
+    for i in range(3):
+        pack_copy(i).wait()
+        weight_copy(i).wait()
+
+    @pl.loop(0, n_heads)
+    def _(h):
+        for i in range(7):
+            head_copy(h, i).wait_send()
+
+    @pl.loop(0, chunks)
+    def _(c):
+        pair_copy(c).wait_send()
+        for i in range(2):
+            turn_copy(c, i).wait_send()
+            side_copy(c, i).wait_send()
+
+
+def attention(qkv, latent, out_weight, modulation, pack, weights):
+    tokens, width = latent.shape
+    chunks = 8
+    F = width // chunks
+    group = out_weight.shape[0]
+    window = 8 * tokens
+    bf, f32 = jnp.bfloat16, jnp.float32
+    dma = pltpu.SemaphoreType.DMA
+    vmem = pl.BlockSpec(memory_space=pltpu.VMEM)
+    hbm = pl.BlockSpec(memory_space=pl.ANY)
+    outs = pl.pallas_call(
+        functools.partial(attention_kernel, chunks),
+        out_shape=[
+            jax.ShapeDtypeStruct((tokens, width), bf),
+            jax.ShapeDtypeStruct((tokens, width), f32),
+            jax.ShapeDtypeStruct((4,) + pack.shape, f32),
+        ]
+        + [jax.ShapeDtypeStruct(w.shape, bf) for w in weights],
+        in_specs=[hbm] + [vmem] * 3 + [hbm] * 4,
+        out_specs=[vmem] * 2 + [hbm] * 4,
+        scratch_shapes=[
+            pltpu.VMEM((group // HD, 3, window, HD), bf),
+            pltpu.VMEM((window, 2 * HD), bf),
+            pltpu.VMEM((2, window // 2, group), bf),
+            pltpu.VMEM((chunks, window // 2, F), bf),
+            pltpu.VMEM((chunks, window // 2, F), bf),
+            pltpu.VMEM((chunks, 2, tokens, F // 2), bf),
+            pltpu.VMEM((chunks, 2, tokens, F // 2), bf),
+            pltpu.VMEM((chunks, 2, tokens, F), f32),
+            pltpu.VMEM((chunks, 2, tokens, F), bf),
+            pltpu.VMEM((chunks, 2, tokens, F), bf),
+            pltpu.VMEM((chunks, tokens, F), f32),
+            dma((4, 7)), dma((4, 7)), dma((4,)),
+            dma((chunks,)), dma((chunks,)),
+            dma((chunks, 2)), dma((chunks, 2)),
+            dma((chunks, 2)), dma((chunks, 2)),
+            dma((3,)), dma((3,)), dma((3,)), dma((3,)), dma,
+        ],
+        compiler_params=pltpu.CompilerParams(
+            collective_id=1, has_side_effects=True, vmem_limit_bytes=60 * 1024 * 1024
+        ),
+        cost_estimate=pl.CostEstimate(flops=6_500_000_000, bytes_accessed=40_000_000, transcendentals=4_200_000),
+        name="attention",
+    )(qkv, latent, out_weight, modulation, pack, *weights)
+    return outs[0], outs[1], outs[2], outs[3:]
 
 
 def expert_kernel(
@@ -310,38 +537,14 @@
     up_weight,
     down_weight,
 ):
-    n_sp = lax.axis_size("sp")
     tokens = latent.shape[1]
-    group_heads = out_weight.shape[0] // HD
-    window_len = tokens * n_sp
-    core = lax.axis_index("sp") % 2
-
-    swap = [(i, i ^ 1) for i in range(n_sp)]
-    weights = []
-    for w in (gate_weight[0], up_weight[0], down_weight[0]):
-        weights += [w, lax.ppermute(w, "sp", swap)]
-
+    weights = [gate_weight[0], up_weight[0], down_weight[0]]
     cells = (route_experts[0] * CAP + route_slots[0]).astype(jnp.float32)
     pack = jnp.concatenate([cells, route_gates[0], jnp.zeros((tokens, 4), jnp.float32)], axis=1).T
-    packs = lax.all_gather(pack, "sp").reshape(n_sp // 2, 2, 8, tokens)
-    packs = lax.dynamic_index_in_dim(packs, core, 1, keepdims=False)
-
-    packed = attention_in[0].reshape(tokens, 3, n_sp, group_heads, HD)
-    attended = attend(lax.all_to_all(packed, "sp", split_axis=2, concat_axis=0, tiled=True))
-    flat_heads = attended.reshape(window_len, group_heads * HD)
-    projected = lax.psum_scatter(
-        jnp.dot(flat_heads, out_weight, preferred_element_type=jnp.float32).astype(jnp.bfloat16),
-        "sp",
-        scatter_dimension=0,
-        tiled=True,
-    ).astype(jnp.float32)
-    residual = latent[0].astype(jnp.float32) + modulation[0] * projected
-    row_mean = jnp.mean(residual, axis=-1, keepdims=True)
-    centered = residual - row_mean
-    variance = jnp.mean(centered * centered, axis=-1, keepdims=True)
-    normed = centered * lax.rsqrt(variance + 1e-06)
-    moe_in = (normed * (1.0 + modulation[2]) + modulation[1]).astype(jnp.bfloat16)
-    return experts(moe_in, residual, modulation[3:4], packs, weights)[None]
+    qkv = jnp.transpose(attention_in[0], (1, 0, 2))
+    moe_in, residual, packs, far = attention(qkv, latent[0], out_weight, modulation, pack, weights)
+    both = [w for pair in zip(weights, far) for w in pair]
+    return experts(moe_in, residual, modulation[3:4], packs, both)[None]
 
 
 def solution(mesh):

time: 356 us -> 277 us (0.78)
  the two profiles are of different devices: /device:TPU:1 before, /device:TPU:26 now
where the time goes in v2:
time: 277 us
  Pallas kernels  271 us (98%)
  local copies, waits for them, and re-layouts  3.83 us (1%)
    pallas_call x1, Pallas kernels, experts(): pl.pallas_call(functools.partial(expert_kernel, chunks), out_shape=jax.Sh...  182 us
    pallas_call x1, Pallas kernels, attention(): pl.pallas_call(functools.partial(attention_kernel, chunks), out_shape=[ja...  89.2 us

profile of v2, /device:TPU:26, one launch (start us, length us, event | category | flops | bytes accessed | tf_op | source)
XLA Modules:
  0.0 276.7 jit_solution(10514066670571433352)
XLA Ops:
  0.0 0.1 pad.2.clone
  0.1 0.7 convert_bitcast_fusion
  0.8 1.3 maximum_bitcast_fusion.pack_ref
  2.1 1.5 slice.3.gate_ref
  3.6 89.2 %attention.1 = (bf16[128,4096]{1,0:T(8,128)(2,1)}, f32[128,4096]{1,0:T(8,128)}, f32[4,8,128]{2,1,0:T(8,128)}, bf16[4096,512]{1,0:T(8,128)(2,1)}, bf16[4096,512]{1,0:T(8,128)(2,1)}, /*index=5*/bf16[512,4096]{1,0:T(8,128)(2,1)}) custom-call(bf16[3,128,4096]{2,1,0:T(8,128)(2,1)} %bitcast.21, bf16[128,4096]{1,0:T(8,128)(2,1)} %bitcast.22, ...), custom_call_target="tpu_custom_call" | custom-call | flops 6499999744 | bytes 40000000 | tf_op jit(solution)/shard_map/attention/pallas_call | solution.py:231
  92.8 181.6 %experts.1 = bf16[128,4096]{1,0:T(8,128)(2,1)} custom-call(bf16[128,4096]{1,0:T(8,128)(2,1)} %get-tuple-element.11.moe_ref, f32[128,4096]{1,0:T(8,128)} %get-tuple-element.12.res_ref, f32[1,4096]{1,0:T(1,128)} %slice.3.gate_ref, f32[4,8,128]{2,1,0:T(8,128)} %get-tuple-element.13.packs_ref, bf16[4096,512]{1,0:T(8,128)(2,1)} %bitcast.16, ...), custom_call_target="tpu_custom_call" | custom-call | flops 25999998976 | bytes 40000000 | tf_op jit(solution)/shard_map/experts/pallas_call | solution.py:494
  274.4 2.3 copy.12
  (1 shorter events, 0.0 us)

commit v3 on v2

v3 whole, which is shorter than its diff:
```python
import functools
import math

import jax
import jax.numpy as jnp
from jax import lax
from jax.experimental import pallas as pl
from jax.experimental.pallas import tpu as pltpu
from jax.sharding import PartitionSpec as P

HD = 128
MESH = pl.DeviceIdType.MESH

PLANE = (
    (1, 0), (0, 1), (3, 0), (0, 3), (1, 1), (3, 3), (2, 0), (0, 2),
    (1, 3), (3, 1), (2, 1), (1, 2), (2, 3), (3, 2), (2, 2),
)
LINE = (1, 3, 2)
CAP = 12
BLOCK_SLOTS = 4 * CAP
FAR_LATE = 8
W_SLOTS = 3
D_SLOTS = 5
SHARED = 3
SET_ORDER = (1, 2, 4, 7, 3, 6, 5)


def attention_kernel(
    chunks,
    qkv_ref, latent_ref, wo_ref, mod_ref, experts_ref, slots_ref, gates_ref, wg_ref, wu_ref, wd_ref,
    moe_ref, res_ref, packs_ref, wg_far, wu_far, wd_far,
    pack_ref, heads, values, att, pair_out, pair_in, turn_out, turn_in, side, side_out, side_in, own,
    q_s, q_r, q_l, p_s, p_r, t_s, t_r, s_s, s_r, w_s, w_r, k_s, k_r, k_l,
):
    sp, ep = lax.axis_index("sp"), lax.axis_index("ep")
    x, core = sp // 2, sp % 2
    n_heads, _, window, hd = heads.shape
    tokens = window // 8
    F = wo_ref.shape[1] // chunks
    H = F // 2
    f32, bf = jnp.float32, jnp.bfloat16

    def x_peer(d):
        return (x + d) % 4

    def x_dev(d):
        return (x_peer(d) * 2 + core, ep)

    partner = (x * 2 + 1 - core, ep)
    others = [(d, k) for d in (2, 1, 3, 0) for k in (0, 1) if (d, k) != (0, 0)]

    def other(i):
        d, k = others[i]
        return x_peer(d) * 2 + (core + k) % 2

    def cols(c):
        return pl.ds(pl.multiple_of(c * F, F), F)

    def block(s):
        return pl.ds(pl.multiple_of(s * tokens, tokens), tokens)

    def head_cols(s, h):
        return pl.ds(pl.multiple_of((s * n_heads + h) * hd, hd), hd)

    def head_copy(h, i):
        to = other(i)
        return pltpu.make_async_remote_copy(
            qkv_ref.at[:, :, head_cols(to, h)], heads.at[h, :, block(sp), :], q_s.at[h, i], q_r.at[h, i],
            device_id=(to, ep), device_id_type=MESH,
        )

    def head_local(h):
        return pltpu.make_async_copy(
            qkv_ref.at[:, :, head_cols(sp, h)], heads.at[h, :, block(sp), :], q_l.at[h]
        )

    def weight_copy(i):
        src, dst = ((wg_ref, wg_far), (wu_ref, wu_far), (wd_ref, wd_far))[i]
        return pltpu.make_async_remote_copy(
            src, dst, w_s.at[i], w_r.at[i], device_id=partner, device_id_type=MESH
        )

    def pack_copy(i):
        return pltpu.make_async_remote_copy(
            pack_ref, packs_ref.at[x], k_s.at[i], k_r.at[i], device_id=x_dev(LINE[i]), device_id_type=MESH
        )

    pack_local = pltpu.make_async_copy(pack_ref, packs_ref.at[x], k_l)

    def pair_copy(c):
        return pltpu.make_async_remote_copy(
            pair_out.at[c], pair_in.at[c], p_s.at[c], p_r.at[c], device_id=partner, device_id_type=MESH
        )

    def turn_copy(c, i):
        return pltpu.make_async_remote_copy(
            turn_out.at[c, i], turn_in.at[c, i], t_s.at[c, i], t_r.at[c, i],
            device_id=x_dev((3, 1)[i]), device_id_type=MESH,
        )

    def side_copy(c, i):
        return pltpu.make_async_remote_copy(
            side_out.at[c, i], side_in.at[c, i], s_s.at[c, i], s_r.at[c, i],
            device_id=x_dev((3, 1)[i]), device_id_type=MESH,
        )

    barrier = pltpu.get_barrier_semaphore()
    for i in range(7):
        pl.semaphore_signal(barrier, inc=1, device_id=(other(i), ep), device_id_type=MESH)
    for h in range(n_heads):
        head_local(h).start()
    pack_ref[0:2, :] = (experts_ref[...] * CAP + slots_ref[...]).astype(f32)
    pack_ref[2:4, :] = gates_ref[...]
    pack_ref[4:8, :] = jnp.zeros((4, tokens), f32)
    pack_local.start()
    pl.semaphore_wait(barrier, 7)

    @pl.loop(0, n_heads)
    def _(h):
        for i in range(7):
            head_copy(h, i).start()

    for i in range(3):
        pack_copy(i).start()
    for i in range(3):
        weight_copy(i).start()

    values[:, hd:] = jnp.ones((window, hd), bf)
    factor = math.log2(math.e) / math.sqrt(hd)
    q_tile = 2 * tokens

    @pl.loop(0, n_heads)
    def _(h):
        head_local(h).wait()
        for i in range(7):
            head_copy(h, i).wait_recv()
        values[:, :hd] = heads[h, 2]

        @pl.loop(0, window // q_tile)
        def _(m):
            at = pl.ds(pl.multiple_of(m * q_tile, q_tile), q_tile)
            scores = lax.dot_general(
                heads[h, 0, at, :], heads[h, 1], (((1,), (1,)), ((), ())), preferred_element_type=f32
            )
            top = jnp.max(scores, axis=1, keepdims=True)
            lifted = jnp.exp2((scores - top) * factor).astype(bf)
            mixed = jnp.dot(lifted, values[...], preferred_element_type=f32)
            out = (mixed[:, :hd] / mixed[:, hd:]).astype(bf)
            to = (block(m), pl.ds(pl.multiple_of(h * hd, hd), hd))
            att[0, to[0], to[1]] = out[:tokens]
            att[1, to[0], to[1]] = out[tokens:]

    far_at = (1 - core) * FAR_LATE
    sum_at = 1 + core * (chunks - 1)

    @pl.loop(0, 2 * chunks + 5)
    def _(step):
        @pl.when((step >= far_at) & (step < far_at + chunks))
        def _():
            c = step - far_at
            far = jnp.dot(att[1 - core], wo_ref[:, cols(c)], preferred_element_type=f32)
            pair_out[c] = far.astype(bf)
            pair_copy(c).start()

        @pl.when((step >= sum_at) & (step < sum_at + chunks))
        def _():
            c = step - sum_at
            pair_copy(c).wait_recv()

            def part(b):
                return jnp.dot(
                    att[core, block(b), :], wo_ref[:, cols(c)], preferred_element_type=f32
                ) + pair_in[c, block(b), :].astype(f32)

            over = part(x_peer(2)).astype(bf)
            for i in range(2):
                turn_out[c, i] = over[:, i * H : (i + 1) * H]
                turn_copy(c, i).start()
            side[c, 0] = part(x_peer(3))
            side[c, 1] = part(x_peer(1))
            own[c] = part(x)

        @pl.when((step >= sum_at + 2) & (step < sum_at + chunks + 2))
        def _():
            c = step - sum_at - 2
            for i in range(2):
                turn_copy(c, i).wait_recv()
                near = slice(i * H, (i + 1) * H)
                rest = slice((1 - i) * H, (2 - i) * H)
                side_out[c, i, :, near] = (side[c, i, :, near] + turn_in[c, i].astype(f32)).astype(bf)
                side_out[c, i, :, rest] = side[c, i, :, rest].astype(bf)
                side_copy(c, i).start()

        @pl.when((step >= sum_at + 5) & (step < sum_at + chunks + 5))
        def _():
            c = step - sum_at - 5
            total = own[c]
            for i in range(2):
                side_copy(c, i).wait_recv()
                total = total + side_in[c, i].astype(f32)
            res_ref[:, cols(c)] = latent_ref[:, cols(c)].astype(f32) + mod_ref[0:1, cols(c)] * total

    @pl.loop(0, tokens // 16)
    def _(m):
        at = pl.ds(pl.multiple_of(m * 16, 16), 16)
        rows = res_ref[at, :]
        centered = rows - jnp.mean(rows, axis=1, keepdims=True)
        variance = jnp.mean(centered * centered, axis=1, keepdims=True)
        normed = centered * lax.rsqrt(variance + 1e-06)
        moe_ref[at, :] = (normed * (1.0 + mod_ref[2:3, :]) + mod_ref[1:2, :]).astype(bf)

    pack_local.wait()
    for i in range(3):
        pack_copy(i).wait()
        weight_copy(i).wait()

    @pl.loop(0, n_heads)
    def _(h):
        for i in range(7):
            head_copy(h, i).wait_send()

    @pl.loop(0, chunks)
    def _(c):
        pair_copy(c).wait_send()
        for i in range(2):
            turn_copy(c, i).wait_send()
            side_copy(c, i).wait_send()


def attention(qkv, latent, out_weight, modulation, routes, weights):
    tokens, width = latent.shape
    chunks = 8
    F = width // chunks
    group = out_weight.shape[0]
    window = 8 * tokens
    bf, f32 = jnp.bfloat16, jnp.float32
    dma = pltpu.SemaphoreType.DMA
    vmem = pl.BlockSpec(memory_space=pltpu.VMEM)
    hbm = pl.BlockSpec(memory_space=pl.ANY)
    outs = pl.pallas_call(
        functools.partial(attention_kernel, chunks),
        out_shape=[
            jax.ShapeDtypeStruct((tokens, width), bf),
            jax.ShapeDtypeStruct((tokens, width), f32),
            jax.ShapeDtypeStruct((4, 8, tokens), f32),
        ]
        + [jax.ShapeDtypeStruct(w.shape, bf) for w in weights],
        in_specs=[hbm] + [vmem] * 6 + [hbm] * 3,
        out_specs=[vmem] * 2 + [hbm] * 4,
        scratch_shapes=[
            pltpu.VMEM((8, tokens), f32),
            pltpu.VMEM((group // HD, 3, window, HD), bf),
            pltpu.VMEM((window, 2 * HD), bf),
            pltpu.VMEM((2, window // 2, group), bf),
            pltpu.VMEM((chunks, window // 2, F), bf),
            pltpu.VMEM((chunks, window // 2, F), bf),
            pltpu.VMEM((chunks, 2, tokens, F // 2), bf),
            pltpu.VMEM((chunks, 2, tokens, F // 2), bf),
            pltpu.VMEM((chunks, 2, tokens, F), f32),
            pltpu.VMEM((chunks, 2, tokens, F), bf),
            pltpu.VMEM((chunks, 2, tokens, F), bf),
            pltpu.VMEM((chunks, tokens, F), f32),
            dma((4, 7)), dma((4, 7)), dma((4,)),
            dma((chunks,)), dma((chunks,)),
            dma((chunks, 2)), dma((chunks, 2)),
            dma((chunks, 2)), dma((chunks, 2)),
            dma((3,)), dma((3,)), dma((3,)), dma((3,)), dma,
        ],
        compiler_params=pltpu.CompilerParams(
            collective_id=1, has_side_effects=True, vmem_limit_bytes=60 * 1024 * 1024
        ),
        cost_estimate=pl.CostEstimate(flops=6_500_000_000, bytes_accessed=40_000_000, transcendentals=4_200_000),
        name="attention",
    )(qkv, latent, out_weight, modulation, *routes, *weights)
    return outs[0], outs[1], outs[2], outs[3:]


def expert_kernel(
    chunks,
    moe_ref, res_ref, mod_ref, packs_ref, wg_own, wg_far, wu_own, wu_far, wd_own, wd_far,
    out_ref,
    tok, send, recv, back, mate, turn_in, side_in, acc_g, acc_u, act, wg, wu, wd, spread, merge, part_ref,
    a_s, a_r, f_s, f_r, d_s, d_r, r_s, r_r, m_s, m_r, n_s, n_r, t_s, t_r, s_s, s_r, w_sem, wd_sem,
):
    sp, ep = lax.axis_index("sp"), lax.axis_index("ep")
    x, core = sp // 2, sp % 2
    z, y = ep // 4, ep % 4
    mine = x % 2
    F = tok.shape[3]
    H = F // 2
    half = wg_own.shape[1]
    rows = send.shape[2]
    tokens = tok.shape[2]
    f32, bf = jnp.float32, jnp.bfloat16

    def x_dev(d):
        return (((x + d) % 4) * 2 + core, ep)

    mate_dev = ((x + 1 - 2 * mine) * 2 + core, ep)

    def offset(m, i):
        return i // 2, (2 * (i % 2) + (i // 2) % 2 + m) % 4

    def plane_dev(m, i, sign):
        dz, dy = offset(m, i)
        return (sp, ((z + sign * dz + 4) % 4) * 4 + (y + sign * dy + 4) % 4)

    seats = [(q // 8, q % 8) for q in range(1, 16)]
    order = [next(q for q in seats if offset(*q) == o) for o in PLANE]

    barrier = pltpu.get_barrier_semaphore()
    for d in LINE:
        pl.semaphore_signal(barrier, inc=1, device_id=x_dev(d), device_id_type=MESH)
    for m, i in order:
        pl.semaphore_signal(barrier, inc=1, device_id=plane_dev(m, i, 1), device_id_type=MESH)

    def shared(c):
        return (c % 2 == 1) & (c < 2 * SHARED)

    def cols(c):
        return pl.ds(pl.multiple_of(c * F, F), F)

    def seat(i):
        return pl.ds(i * BLOCK_SLOTS, BLOCK_SLOTS)

    def w_copies(k):
        s = k % W_SLOTS
        return [
            pltpu.make_async_copy(src.at[cols(k), :], dst.at[s, :, pl.ds(at, half)], w_sem.at[s, i])
            for i, (src, dst, at) in enumerate(
                ((wg_own, wg, 0), (wg_far, wg, half), (wu_own, wu, 0), (wu_far, wu, half))
            )
        ]

    def wd_copies(k):
        s = k % D_SLOTS
        return [
            pltpu.make_async_copy(src.at[:, cols(k)], wd.at[s, pl.ds(at, half), :], wd_sem.at[s, i])
            for i, (src, at) in enumerate(((wd_own, 0), (wd_far, half)))
        ]

    def near_copy(c, i):
        return pltpu.make_async_remote_copy(
            moe_ref.at[:, cols(c)], tok.at[c, x], a_s.at[c, i], a_r.at[c, i],
            device_id=x_dev((1, 3)[i]), device_id_type=MESH,
        )

    def pass_copy(c, i):
        block = tok.at[c, (x + (1, 3)[i]) % 4, :, pl.ds(i * H, H)]
        return pltpu.make_async_remote_copy(
            block, block, f_s.at[c, i], f_r.at[c, i], device_id=x_dev((3, 1)[i]), device_id_type=MESH
        )

    def seat_copy(c, m, i, dst, s_sem, r_sem, sign):
        return pltpu.make_async_remote_copy(
            send.at[c, m, seat(i)], dst.at[c, m, seat(i)], s_sem.at[c, m * 8 + i], r_sem.at[c, m * 8 + i],
            device_id=plane_dev(m, i, sign), device_id_type=MESH,
        )

    def seat_copies(c, way, act_on):
        args = (recv, d_s, d_r, 1) if way == 0 else (back, r_s, r_r, -1)

        @pl.when(shared(c))
        def _():
            for i in SET_ORDER:
                act_on(seat_copy(c, mine, i, *args))

            @pl.when(mine == 1)
            def _():
                act_on(seat_copy(c, mine, 0, *args))

        @pl.when(jnp.logical_not(shared(c)))
        def _():
            for m, i in order:
                act_on(seat_copy(c, m, i, *args))

    def start(copy):
        copy.start()

    def wait_recv(copy):
        copy.wait_recv()

    def wait_send(copy):
        copy.wait_send()

    def mate_rows(c):
        return pltpu.make_async_remote_copy(
            recv.at[c, mine], recv.at[c, mine], m_s.at[c], m_r.at[c], device_id=mate_dev, device_id_type=MESH
        )

    def mate_sums(c):
        return pltpu.make_async_remote_copy(
            send.at[c, 1 - mine], mate.at[c // 2], n_s.at[c], n_r.at[c], device_id=mate_dev, device_id_type=MESH
        )

    def turn_copy(c, i):
        return pltpu.make_async_remote_copy(
            tok.at[c, 0, :, pl.ds(i * H, H)], turn_in.at[c, i], t_s.at[c, i], t_r.at[c, i],
            device_id=x_dev((3, 1)[i]), device_id_type=MESH,
        )

    def side_copy(c, i):
        return pltpu.make_async_remote_copy(
            tok.at[c, 1 + i], side_in.at[c, i], s_s.at[c, i], s_r.at[c, i],
            device_id=x_dev((3, 1)[i]), device_id_type=MESH,
        )

    pl.semaphore_wait(barrier, len(LINE) + len(PLANE))

    @pl.loop(0, chunks)
    def _(c):
        for i in range(2):
            near_copy(c, i).start()

    for k in range(W_SLOTS):
        for cp in w_copies(k):
            cp.start()
    for k in range(D_SLOTS):
        for cp in wd_copies(k):
            cp.start()

    row = lax.broadcasted_iota(jnp.int32, (rows, 1), 0)
    place, rest = row // BLOCK_SLOTS, row % BLOCK_SLOTS
    block, slot = rest // CAP, rest % CAP
    for m in range(2):
        dz, dy = offset(m, place)
        pair = ((z + dz) % 4) * 4 + (y + dy) % 4
        wanted = (2 * pair + x // 2) * CAP + slot
        for b in range(4):
            at = slice(b * tokens, (b + 1) * tokens)
            key = jnp.where(block == b, wanted, -1).astype(f32)
            first = packs_ref[b, 0:1, :] == key
            second = packs_ref[b, 1:2, :] == key
            spread[m, :, at] = jnp.where(first | second, 1.0, 0.0).astype(bf)
            weight = jnp.where(first, packs_ref[b, 2:3, :], 0.0) + jnp.where(second, packs_ref[b, 3:4, :], 0.0)
            merge[m, at, :] = weight.T.astype(bf)

    acc_g[...] = jnp.zeros_like(acc_g)
    acc_u[...] = jnp.zeros_like(acc_u)

    def pass_on(c):
        for i in range(2):
            near_copy(c, 1 - i).wait_recv()
            pass_copy(c, i).start()

    pass_on(0)

    @pl.loop(0, chunks + 3)
    def _(step):
        @pl.when(step + 1 < chunks)
        def _():
            pass_on(step + 1)

        @pl.when(step < chunks)
        def _():
            c = step
            tok[c, x] = moe_ref[:, cols(c)]
            for i in range(2):
                pass_copy(c, i).wait_recv()
            lines = tok[c].reshape(4 * tokens, F)

            @pl.loop(0, 2)
            def _(m):
                @pl.when(jnp.logical_not(shared(c)) | (m == mine))
                def _():
                    send[c, m] = jnp.dot(spread[m], lines, preferred_element_type=f32).astype(bf)

            seat_copies(c, 0, start)

            @pl.when(jnp.logical_not(shared(c)) | (mine == 0))
            def _():
                recv[c, 0, seat(0)] = send[c, 0, seat(0)]

        @pl.when(step >= 3)
        def _():
            k = step - 3
            s = k % W_SLOTS
            for cp in w_copies(k):
                cp.wait()

            @pl.when(shared(k))
            def _():
                mate_rows(k).wait_recv()

            @pl.when(jnp.logical_not(shared(k)))
            def _():
                for m, i in order:
                    seat_copy(k, m, i, recv, d_s, d_r, 1).wait_recv()

            @pl.loop(0, 2)
            def _(m):
                lines = recv[k, m]
                acc_g[m] += jnp.dot(lines, wg[s], preferred_element_type=f32)
                acc_u[m] += jnp.dot(lines, wu[s], preferred_element_type=f32)

            @pl.when(k + W_SLOTS < chunks)
            def _():
                for cp in w_copies(k + W_SLOTS):
                    cp.start()

        @pl.when((step >= 2) & shared(step - 2))
        def _():
            k = step - 2
            for i in SET_ORDER:
                seat_copy(k, mine, i, recv, d_s, d_r, 1).wait_recv()

            @pl.when(mine == 1)
            def _():
                seat_copy(k, mine, 0, recv, d_s, d_r, 1).wait_recv()

            mate_rows(k).start()

    @pl.loop(0, 2 * rows // 64)
    def _(t):
        m, at = t // (rows // 64), pl.ds(pl.multiple_of((t % (rows // 64)) * 64, 64), 64)
        g = acc_g[m, at, :]
        act[m, at, :] = (g / (1.0 + jnp.exp(-g)) * acc_u[m, at, :]).astype(bf)

    def part(k, b):
        at = pl.ds(pl.multiple_of(b * tokens, tokens), tokens)
        part_ref[...] = jnp.dot(merge[mine, at, :], back[k, mine], preferred_element_type=f32)

        @pl.when(jnp.logical_not(shared(k)))
        def _():
            part_ref[...] += jnp.dot(merge[1 - mine, at, :], back[k, 1 - mine], preferred_element_type=f32)

        return part_ref[...]

    @pl.loop(0, chunks + 6)
    def _(step):
        @pl.when(step < chunks)
        def _():
            c = step
            s = c % D_SLOTS
            for cp in wd_copies(c):
                cp.wait()
            seat_copies(c, 0, wait_send)

            @pl.loop(0, 2)
            def _(m):
                @pl.when(jnp.logical_not(shared(c)) | (m != mine))
                def _():
                    send[c, m] = jnp.dot(act[m], wd[s], preferred_element_type=f32).astype(bf)

            @pl.when(shared(c))
            def _():
                mate_sums(c).start()

            @pl.when(jnp.logical_not(shared(c)))
            def _():
                for m, i in order:
                    seat_copy(c, m, i, back, r_s, r_r, -1).start()
                back[c, 0, seat(0)] = send[c, 0, seat(0)]

        @pl.when((step >= 1) & (step < chunks + 1))
        def _():
            k = step - 1

            @pl.when(shared(k))
            def _():
                mate_sums(k).wait_recv()
                both = jnp.dot(act[mine], wd[k % D_SLOTS], preferred_element_type=f32) + mate[k // 2].astype(f32)
                send[k, mine] = both.astype(bf)
                for i in SET_ORDER:
                    seat_copy(k, mine, i, back, r_s, r_r, -1).start()

                @pl.when(mine == 1)
                def _():
                    seat_copy(k, mine, 0, back, r_s, r_r, -1).start()

                @pl.when(mine == 0)
                def _():
                    back[k, 0, seat(0)] = send[k, 0, seat(0)]

            @pl.when(k + D_SLOTS < chunks)
            def _():
                for cp in wd_copies(k + D_SLOTS):
                    cp.start()

        @pl.when((step >= 3) & (step < chunks + 3))
        def _():
            k = step - 3
            seat_copies(k, 1, wait_recv)
            for i in range(2):
                pass_copy(k, i).wait_send()
            tok[k, 0] = part(k, (x + 2) % 4).astype(bf)
            for i in range(2):
                turn_copy(k, i).start()

        @pl.when((step >= 4) & (step < chunks + 4))
        def _():
            k = step - 4
            for i in range(2):
                near = slice(i * H, (i + 1) * H)
                rest = slice((1 - i) * H, (2 - i) * H)
                side = part(k, (x + (3, 1)[i]) % 4)
                turn_copy(k, i).wait_recv()
                tok[k, 1 + i, :, near] = (side[:, near] + turn_in[k, i].astype(f32)).astype(bf)
                tok[k, 1 + i, :, rest] = side[:, rest].astype(bf)
                side_copy(k, i).start()

        @pl.when(step >= 6)
        def _():
            k = step - 6
            total = part(k, x)
            for i in range(2):
                side_copy(k, i).wait_recv()
                total = total + side_in[k, i].astype(f32)
            out_ref[:, cols(k)] = (res_ref[:, cols(k)] + mod_ref[3:4, cols(k)] * total).astype(out_ref.dtype)

    @pl.loop(0, chunks)
    def _(c):
        for i in range(2):
            near_copy(c, i).wait_send()
            turn_copy(c, i).wait_send()
            side_copy(c, i).wait_send()
        seat_copies(c, 1, wait_send)

        @pl.when(shared(c))
        def _():
            mate_rows(c).wait_send()
            mate_sums(c).wait_send()


def experts(moe_in, residual, modulation, packs, weights):
    tokens, width = moe_in.shape
    chunks = 8
    F = width // chunks
    rows = 8 * BLOCK_SLOTS
    hidden = 2 * weights[0].shape[1]
    bf, f32 = jnp.bfloat16, jnp.float32
    dma = pltpu.SemaphoreType.DMA
    vmem = pl.BlockSpec(memory_space=pltpu.VMEM)
    hbm = pl.BlockSpec(memory_space=pl.ANY)
    return pl.pallas_call(
        functools.partial(expert_kernel, chunks),
        out_shape=jax.ShapeDtypeStruct((tokens, width), bf),
        in_specs=[vmem] * 4 + [hbm] * 6,
        out_specs=vmem,
        scratch_shapes=[
            pltpu.VMEM((chunks, 4, tokens, F), bf),
            pltpu.VMEM((chunks, 2, rows, F), bf),
            pltpu.VMEM((chunks, 2, rows, F), bf),
            pltpu.VMEM((chunks, 2, rows, F), bf),
            pltpu.VMEM((SHARED, rows, F), bf),
            pltpu.VMEM((chunks, 2, tokens, F // 2), bf),
            pltpu.VMEM((chunks, 2, tokens, F), bf),
            pltpu.VMEM((2, rows, hidden), f32),
            pltpu.VMEM((2, rows, hidden), f32),
            pltpu.VMEM((2, rows, hidden), bf),
            pltpu.VMEM((W_SLOTS, F, hidden), bf),
            pltpu.VMEM((W_SLOTS, F, hidden), bf),
            pltpu.VMEM((D_SLOTS, hidden, F), bf),
            pltpu.VMEM((2, rows, 4 * tokens), bf),
            pltpu.VMEM((2, 4 * tokens, rows), bf),
            pltpu.VMEM((tokens, F), f32),
        ]
        + [dma((chunks, 2))] * 4
        + [dma((chunks, 16))] * 4
        + [dma((chunks,))] * 4
        + [dma((chunks, 2))] * 4
        + [dma((W_SLOTS, 4)), dma((D_SLOTS, 2))],
        compiler_params=pltpu.CompilerParams(
            collective_id=0, has_side_effects=True, vmem_limit_bytes=62 * 1024 * 1024
        ),
        cost_estimate=pl.CostEstimate(flops=26_000_000_000, bytes_accessed=40_000_000, transcendentals=800_000),
        name="experts",
    )(moe_in, residual, modulation, packs, *weights)


def local(
    latent,
    attention_in,
    out_weight,
    modulation,
    route_experts,
    route_slots,
    route_gates,
    gate_weight,
    up_weight,
    down_weight,
):
    weights = [gate_weight[0], up_weight[0], down_weight[0]]
    routes = [route_experts[0].T, route_slots[0].T, route_gates[0].T]
    qkv = jnp.transpose(attention_in[0], (1, 0, 2))
    moe_in, residual, packs, far = attention(qkv, latent[0], out_weight, modulation, routes, weights)
    both = [w for pair in zip(weights, far) for w in pair]
    return experts(moe_in, residual, modulation, packs, both)[None]


def solution(mesh):
    return jax.shard_map(
        local,
        mesh=mesh,
        in_specs=(
            P("ep", "sp", None),
            P("ep", "sp", None, None),
            P("sp", None),
            P(),
            P("ep", "sp", None),
            P("ep", "sp", None),
            P("ep", "sp", None),
            P("ep", None, "sp"),
            P("ep", None, "sp"),
            P("ep", "sp", None),
        ),
        out_specs=P("ep", "sp", None),
        check_vma=False,
    )
```

time: 277 us -> 245 us (0.88)
  the two profiles are of different devices: /device:TPU:26 before, /device:TPU:1 now
where the time goes in v3:
time: 245 us
  Pallas kernels  243 us (99%)
    pallas_call x1, Pallas kernels, experts(): pl.pallas_call(functools.partial(expert_kernel, chunks), out_shape=jax.Sh...  151 us
    pallas_call x1, Pallas kernels, attention(): pl.pallas_call(functools.partial(attention_kernel, chunks), out_shape=[ja...  92.3 us

profile of v3, /device:TPU:1, one launch (start us, length us, event | category | flops | bytes accessed | tf_op | source)
XLA Modules:
  0.0 245.1 jit_solution(10274052379425010642)
XLA Ops:
  0.0 92.3 %attention.1 = (bf16[128,4096]{1,0:T(8,128)(2,1)}, f32[128,4096]{1,0:T(8,128)}, f32[4,8,128]{2,1,0:T(8,128)}, bf16[4096,512]{1,0:T(8,128)(2,1)}, bf16[4096,512]{1,0:T(8,128)(2,1)}, /*index=5*/bf16[512,4096]{1,0:T(8,128)(2,1)}) custom-call(bf16[3,128,4096]{2,1,0:T(8,128)(2,1)} %bitcast.24, bf16[128,4096]{1,0:T(8,128)(2,1)} %bitcast.25, ...), custom_call_target="tpu_custom_call" | custom-call | flops 6499999744 | bytes 40000000 | tf_op jit(solution)/shard_map/attention/pallas_call | solution.py:240
  92.3 150.5 %experts.1 = bf16[128,4096]{1,0:T(8,128)(2,1)} custom-call(bf16[128,4096]{1,0:T(8,128)(2,1)} %get-tuple-element.11.moe_ref, f32[128,4096]{1,0:T(8,128)} %get-tuple-element.12.res_ref, f32[4,4096]{1,0:T(4,128)} %mod_ref.3, f32[4,8,128]{2,1,0:T(8,128)} %get-tuple-element.13.packs_ref, bf16[4096,512]{1,0:T(8,128)(2,1)} %bitcast.19, ...), custom_call_target="tpu_custom_call" | custom-call | flops 25999998976 | bytes 40000000 | tf_op jit(solution)/shard_map/experts/pallas_call | solution.py:635
  242.8 2.3 copy.12

commit v4 on v3

--- a/solution.py
+++ b/solution.py
@@ -27,10 +27,10 @@
 
 def attention_kernel(
     chunks,
-    qkv_ref, latent_ref, wo_ref, mod_ref, experts_ref, slots_ref, gates_ref, wg_ref, wu_ref, wd_ref,
-    moe_ref, res_ref, packs_ref, wg_far, wu_far, wd_far,
-    pack_ref, heads, values, att, pair_out, pair_in, turn_out, turn_in, side, side_out, side_in, own,
-    q_s, q_r, q_l, p_s, p_r, t_s, t_r, s_s, s_r, w_s, w_r, k_s, k_r, k_l,
+    qkv_ref, latent_hbm, wo_hbm, mod_ref, experts_ref, slots_ref, gates_ref, wg_ref, wu_ref, wd_ref,
+    moe_hbm, res_hbm, packs_ref, wg_far, wu_far, wd_far,
+    latent_ref, wo_ref, moe_ref, res_ref, pack_ref, heads, values, att, pair_out, pair_in, turn_out, turn_in, side, side_out, side_in, own,
+    q_s, q_r, q_l, p_s, p_r, t_s, t_r, s_s, s_r, w_s, w_r, k_s, k_r, k_l, in_sem, moe_sem, res_sem,
 ):
     sp, ep = lax.axis_index("sp"), lax.axis_index("ep")
     x, core = sp // 2, sp % 2
@@ -103,6 +103,18 @@
             side_out.at[c, i], side_in.at[c, i], s_s.at[c, i], s_r.at[c, i],
             device_id=x_dev((3, 1)[i]), device_id_type=MESH,
         )
+
+    loads = [
+        pltpu.make_async_copy(wo_hbm, wo_ref, in_sem.at[0]),
+        pltpu.make_async_copy(latent_hbm, latent_ref, in_sem.at[1]),
+    ]
+
+    def moe_copy(m):
+        at = pl.ds(pl.multiple_of(m * 16, 16), 16)
+        return pltpu.make_async_copy(moe_ref.at[at, :], moe_hbm.at[at, :], moe_sem.at[m])
+
+    def res_copy(c):
+        return pltpu.make_async_copy(res_ref.at[:, cols(c)], res_hbm.at[:, cols(c)], res_sem.at[c])
 
     barrier = pltpu.get_barrier_semaphore()
     for i in range(7):
@@ -125,6 +137,8 @@
     for i in range(3):
         weight_copy(i).start()
 
+    for cp in loads:
+        cp.start()
     values[:, hd:] = jnp.ones((window, hd), bf)
     factor = math.log2(math.e) / math.sqrt(hd)
     q_tile = 2 * tokens
@@ -150,6 +164,9 @@
             att[0, to[0], to[1]] = out[:tokens]
             att[1, to[0], to[1]] = out[tokens:]
 
+    for cp in loads:
+        cp.wait()
+
     far_at = (1 - core) * FAR_LATE
     sum_at = 1 + core * (chunks - 1)
 
@@ -199,6 +216,7 @@
                 side_copy(c, i).wait_recv()
                 total = total + side_in[c, i].astype(f32)
             res_ref[:, cols(c)] = latent_ref[:, cols(c)].astype(f32) + mod_ref[0:1, cols(c)] * total
+            res_copy(c).start()
 
     @pl.loop(0, tokens // 16)
     def _(m):
@@ -208,6 +226,11 @@
         variance = jnp.mean(centered * centered, axis=1, keepdims=True)
         normed = centered * lax.rsqrt(variance + 1e-06)
         moe_ref[at, :] = (normed * (1.0 + mod_ref[2:3, :]) + mod_ref[1:2, :]).astype(bf)
+        moe_copy(m).start()
+
+    @pl.loop(0, tokens // 16)
+    def _(m):
+        moe_copy(m).wait()
 
     pack_local.wait()
     for i in range(3):
@@ -221,6 +244,7 @@
 
     @pl.loop(0, chunks)
     def _(c):
+        res_copy(c).wait()
         pair_copy(c).wait_send()
         for i in range(2):
             turn_copy(c, i).wait_send()
@@ -245,9 +269,13 @@
             jax.ShapeDtypeStruct((4, 8, tokens), f32),
         ]
         + [jax.ShapeDtypeStruct(w.shape, bf) for w in weights],
-        in_specs=[hbm] + [vmem] * 6 + [hbm] * 3,
-        out_specs=[vmem] * 2 + [hbm] * 4,
+        in_specs=[hbm] * 3 + [vmem] * 4 + [hbm] * 3,
+        out_specs=[hbm] * 6,
         scratch_shapes=[
+            pltpu.VMEM((tokens, width), bf),
+            pltpu.VMEM((group, width), bf),
+            pltpu.VMEM((tokens, width), bf),
+            pltpu.VMEM((tokens, width), f32),
             pltpu.VMEM((8, tokens), f32),
             pltpu.VMEM((group // HD, 3, window, HD), bf),
             pltpu.VMEM((window, 2 * HD), bf),
@@ -265,6 +293,7 @@
             dma((chunks, 2)), dma((chunks, 2)),
             dma((chunks, 2)), dma((chunks, 2)),
             dma((3,)), dma((3,)), dma((3,)), dma((3,)), dma,
+            dma((2,)), dma((tokens // 16,)), dma((chunks,)),
         ],
         compiler_params=pltpu.CompilerParams(
             collective_id=1, has_side_effects=True, vmem_limit_bytes=60 * 1024 * 1024
@@ -277,10 +306,10 @@
 
 def expert_kernel(
     chunks,
-    moe_ref, res_ref, mod_ref, packs_ref, wg_own, wg_far, wu_own, wu_far, wd_own, wd_far,
+    moe_ref, res_hbm, mod_ref, packs_ref, wg_own, wg_far, wu_own, wu_far, wd_own, wd_far,
     out_ref,
-    tok, send, recv, back, mate, turn_in, side_in, acc_g, acc_u, act, wg, wu, wd, spread, merge, part_ref,
-    a_s, a_r, f_s, f_r, d_s, d_r, r_s, r_r, m_s, m_r, n_s, n_r, t_s, t_r, s_s, s_r, w_sem, wd_sem,
+    tok, send, recv, back, mate, turn_in, side_in, acc_g, acc_u, act, wg, wu, wd, spread, merge, part_ref, res_ref,
+    a_s, a_r, f_s, f_r, d_s, d_r, r_s, r_r, m_s, m_r, n_s, n_r, t_s, t_r, s_s, s_r, w_sem, wd_sem, own_sem, res_sem,
 ):
     sp, ep = lax.axis_index("sp"), lax.axis_index("ep")
     x, core = sp // 2, sp % 2
@@ -339,6 +368,11 @@
             for i, (src, at) in enumerate(((wd_own, 0), (wd_far, half)))
         ]
 
+    def own_copy(c):
+        return pltpu.make_async_copy(moe_ref.at[:, cols(c)], tok.at[c, x], own_sem.at[c])
+
+    res_copy = pltpu.make_async_copy(res_hbm, res_ref, res_sem)
+
     def near_copy(c, i):
         return pltpu.make_async_remote_copy(
             moe_ref.at[:, cols(c)], tok.at[c, x], a_s.at[c, i], a_r.at[c, i],
@@ -407,10 +441,14 @@
 
     pl.semaphore_wait(barrier, len(LINE) + len(PLANE))
 
-    @pl.loop(0, chunks)
+    @pl.loop(0, 2)
     def _(c):
         for i in range(2):
             near_copy(c, i).start()
+
+    @pl.loop(0, chunks)
+    def _(c):
+        own_copy(c).start()
 
     for k in range(W_SLOTS):
         for cp in w_copies(k):
@@ -418,6 +456,7 @@
     for k in range(D_SLOTS):
         for cp in wd_copies(k):
             cp.start()
+    res_copy.start()
 
     row = lax.broadcasted_iota(jnp.int32, (rows, 1), 0)
     place, rest = row // BLOCK_SLOTS, row % BLOCK_SLOTS
@@ -443,9 +482,14 @@
             near_copy(c, 1 - i).wait_recv()
             pass_copy(c, i).start()
 
+        @pl.when(c + 2 < chunks)
+        def _():
+            for i in range(2):
+                near_copy(c + 2, i).start()
+
     pass_on(0)
 
-    @pl.loop(0, chunks + 3)
+    @pl.loop(0, chunks + 2)
     def _(step):
         @pl.when(step + 1 < chunks)
         def _():
@@ -454,7 +498,7 @@
         @pl.when(step < chunks)
         def _():
             c = step
-            tok[c, x] = moe_ref[:, cols(c)]
+            own_copy(c).wait()
             for i in range(2):
                 pass_copy(c, i).wait_recv()
             lines = tok[c].reshape(4 * tokens, F)
@@ -510,11 +554,36 @@
 
             mate_rows(k).start()
 
-    @pl.loop(0, 2 * rows // 64)
-    def _(t):
-        m, at = t // (rows // 64), pl.ds(pl.multiple_of((t % (rows // 64)) * 64, 64), 64)
-        g = acc_g[m, at, :]
-        act[m, at, :] = (g / (1.0 + jnp.exp(-g)) * acc_u[m, at, :]).astype(bf)
+    last = chunks - 1
+    for cp in w_copies(last) + wd_copies(0):
+        cp.wait()
+    seat_copies(last, 0, wait_recv)
+    seat_copies(0, 0, wait_send)
+    res_copy.wait()
+
+    @pl.loop(0, 2)
+    def _(m):
+        lines = recv[last, m]
+        acc_g[m] += jnp.dot(lines, wg[last % W_SLOTS], preferred_element_type=f32)
+        acc_u[m] += jnp.dot(lines, wu[last % W_SLOTS], preferred_element_type=f32)
+
+        @pl.loop(0, rows // 64)
+        def _(t):
+            at = pl.ds(pl.multiple_of(t * 64, 64), 64)
+            g = acc_g[m, at, :]
+            act[m, at, :] = (g / (1.0 + jnp.exp(-g)) * acc_u[m, at, :]).astype(bf)
+
+        send[0, m] = jnp.dot(act[m], wd[0], preferred_element_type=f32).astype(bf)
+        for i in SET_ORDER:
+            seat_copy(0, m, i, back, r_s, r_r, -1).start()
+
+        @pl.when(m == 1)
+        def _():
+            seat_copy(0, m, 0, back, r_s, r_r, -1).start()
+
+        @pl.when(m == 0)
+        def _():
+            back[0, 0, seat(0)] = send[0, 0, seat(0)]
 
     def part(k, b):
         at = pl.ds(pl.multiple_of(b * tokens, tokens), tokens)
@@ -528,7 +597,7 @@
 
     @pl.loop(0, chunks + 6)
     def _(step):
-        @pl.when(step < chunks)
+        @pl.when((step >= 1) & (step < chunks))
         def _():
             c = step
             s = c % D_SLOTS
@@ -635,7 +704,7 @@
     return pl.pallas_call(
         functools.partial(expert_kernel, chunks),
         out_shape=jax.ShapeDtypeStruct((tokens, width), bf),
-        in_specs=[vmem] * 4 + [hbm] * 6,
+        in_specs=[hbm] * 2 + [vmem] * 2 + [hbm] * 6,
         out_specs=vmem,
         scratch_shapes=[
             pltpu.VMEM((chunks, 4, tokens, F), bf),
@@ -654,12 +723,13 @@
             pltpu.VMEM((2, rows, 4 * tokens), bf),
             pltpu.VMEM((2, 4 * tokens, rows), bf),
             pltpu.VMEM((tokens, F), f32),
+            pltpu.VMEM((tokens, width), f32),
         ]
         + [dma((chunks, 2))] * 4
         + [dma((chunks, 16))] * 4
         + [dma((chunks,))] * 4
         + [dma((chunks, 2))] * 4
-        + [dma((W_SLOTS, 4)), dma((D_SLOTS, 2))],
+        + [dma((W_SLOTS, 4)), dma((D_SLOTS, 2)), dma((chunks,)), dma],
         compiler_params=pltpu.CompilerParams(
             collective_id=0, has_side_effects=True, vmem_limit_bytes=62 * 1024 * 1024
         ),

time: 245 us -> 236 us (0.963)
  Pallas kernels: 243 us -> 233 us
    pallas_call x1, Pallas kernels: 151 us -> 143 us  [experts(): pl.pallas_call(functools.partial(expert_kernel, chunks), out_shape=jax.Sh...]
    pallas_call x1, Pallas kernels: 92.3 us -> 89.8 us  [attention(): pl.pallas_call(functools.partial(attention_kernel, chunks), out_shape=[ja...]
where the time goes in v4:
time: 236 us
  Pallas kernels  233 us (99%)
    pallas_call x1, Pallas kernels, experts(): pl.pallas_call(functools.partial(expert_kernel, chunks), out_shape=jax.Sh...  143 us
    pallas_call x1, Pallas kernels, attention(): pl.pallas_call(functools.partial(attention_kernel, chunks), out_shape=[ja...  89.8 us

profile of v4, /device:TPU:1, one launch (start us, length us, event | category | flops | bytes accessed | tf_op | source)
XLA Modules:
  0.0 235.6 jit_solution(8990098843443037003)
XLA Ops:
  0.0 89.8 %attention.1 = (bf16[128,4096]{1,0:T(8,128)(2,1)}, f32[128,4096]{1,0:T(8,128)}, f32[4,8,128]{2,1,0:T(8,128)}, bf16[4096,512]{1,0:T(8,128)(2,1)}, bf16[4096,512]{1,0:T(8,128)(2,1)}, /*index=5*/bf16[512,4096]{1,0:T(8,128)(2,1)}) custom-call(bf16[3,128,4096]{2,1,0:T(8,128)(2,1)} %bitcast.24, bf16[128,4096]{1,0:T(8,128)(2,1)} %bitcast.25, ...), custom_call_target="tpu_custom_call" | custom-call | flops 6499999744 | bytes 40000000 | tf_op jit(solution)/shard_map/attention/pallas_call | solution.py:264
  89.8 143.4 %experts.1 = bf16[128,4096]{1,0:T(8,128)(2,1)} custom-call(bf16[128,4096]{1,0:T(8,128)(2,1)} %get-tuple-element.11.moe_ref, f32[128,4096]{1,0:T(8,128)} %get-tuple-element.12.res_hbm, f32[4,4096]{1,0:T(4,128)} %mod_ref.3, f32[4,8,128]{2,1,0:T(8,128)} %get-tuple-element.13.packs_ref, bf16[4096,512]{1,0:T(8,128)(2,1)} %bitcast.19, ...), custom_call_target="tpu_custom_call" | custom-call | flops 25999998976 | bytes 40000000 | tf_op jit(solution)/shard_map/experts/pallas_call | solution.py:704
  233.3 2.3 copy.12

commit v5 on v4

--- a/solution.py
+++ b/solution.py
@@ -12,8 +12,8 @@
 MESH = pl.DeviceIdType.MESH
 
 PLANE = (
-    (1, 0), (0, 1), (3, 0), (0, 3), (1, 1), (3, 3), (2, 0), (0, 2),
-    (1, 3), (3, 1), (2, 1), (1, 2), (2, 3), (3, 2), (2, 2),
+    (2, 2), (1, 0), (0, 1), (3, 0), (0, 3), (2, 1), (1, 2), (2, 3), (3, 2),
+    (1, 1), (3, 3), (2, 0), (0, 2), (1, 3), (3, 1),
 )
 LINE = (1, 3, 2)
 CAP = 12
@@ -170,7 +170,7 @@
     far_at = (1 - core) * FAR_LATE
     sum_at = 1 + core * (chunks - 1)
 
-    @pl.loop(0, 2 * chunks + 5)
+    @pl.loop(0, 2 * chunks + 6)
     def _(step):
         @pl.when((step >= far_at) & (step < far_at + chunks))
         def _():
@@ -197,9 +197,9 @@
             side[c, 1] = part(x_peer(1))
             own[c] = part(x)
 
-        @pl.when((step >= sum_at + 2) & (step < sum_at + chunks + 2))
-        def _():
-            c = step - sum_at - 2
+        @pl.when((step >= sum_at + 3) & (step < sum_at + chunks + 3))
+        def _():
+            c = step - sum_at - 3
             for i in range(2):
                 turn_copy(c, i).wait_recv()
                 near = slice(i * H, (i + 1) * H)
@@ -208,9 +208,9 @@
                 side_out[c, i, :, rest] = side[c, i, :, rest].astype(bf)
                 side_copy(c, i).start()
 
-        @pl.when((step >= sum_at + 5) & (step < sum_at + chunks + 5))
-        def _():
-            c = step - sum_at - 5
+        @pl.when((step >= sum_at + 6) & (step < sum_at + chunks + 6))
+        def _():
+            c = step - sum_at - 6
             total = own[c]
             for i in range(2):
                 side_copy(c, i).wait_recv()

time: 236 us -> 235 us (level)
  no operation moved by 1% of the time
where the time goes in v5:
time: 235 us
  Pallas kernels  232 us (99%)
    pallas_call x1, Pallas kernels, experts(): pl.pallas_call(functools.partial(expert_kernel, chunks), out_shape=jax.Sh...  143 us
    pallas_call x1, Pallas kernels, attention(): pl.pallas_call(functools.partial(attention_kernel, chunks), out_shape=[ja...  89.1 us

profile of v5, /device:TPU:1, one launch (start us, length us, event | category | flops | bytes accessed | tf_op | source)
XLA Modules:
  0.0 234.6 jit_solution(6805394737053733535)
XLA Ops:
  0.0 89.1 %attention.1 = (bf16[128,4096]{1,0:T(8,128)(2,1)}, f32[128,4096]{1,0:T(8,128)}, f32[4,8,128]{2,1,0:T(8,128)}, bf16[4096,512]{1,0:T(8,128)(2,1)}, bf16[4096,512]{1,0:T(8,128)(2,1)}, /*index=5*/bf16[512,4096]{1,0:T(8,128)(2,1)}) custom-call(bf16[3,128,4096]{2,1,0:T(8,128)(2,1)} %bitcast.24, bf16[128,4096]{1,0:T(8,128)(2,1)} %bitcast.25, ...), custom_call_target="tpu_custom_call" | custom-call | flops 6499999744 | bytes 40000000 | tf_op jit(solution)/shard_map/attention/pallas_call | solution.py:264
  89.1 143.2 %experts.1 = bf16[128,4096]{1,0:T(8,128)(2,1)} custom-call(bf16[128,4096]{1,0:T(8,128)(2,1)} %get-tuple-element.11.moe_ref, f32[128,4096]{1,0:T(8,128)} %get-tuple-element.12.res_hbm, f32[4,4096]{1,0:T(4,128)} %mod_ref.3, f32[4,8,128]{2,1,0:T(8,128)} %get-tuple-element.13.packs_ref, bf16[4096,512]{1,0:T(8,128)(2,1)} %bitcast.19, ...), custom_call_target="tpu_custom_call" | custom-call | flops 25999998976 | bytes 40000000 | tf_op jit(solution)/shard_map/experts/pallas_call | solution.py:704
  232.3 2.3 copy.12

commit v6 on v5

--- a/solution.py
+++ b/solution.py
@@ -336,6 +336,8 @@
 
     seats = [(q // 8, q % 8) for q in range(1, 16)]
     order = [next(q for q in seats if offset(*q) == o) for o in PLANE]
+    turned = [next(q for q in seats if offset(*q) == ((4 - o[0]) % 4, (4 - o[1]) % 4)) for o in PLANE]
+    by_core = [(m, jnp.where(core == 0, i, j)) for (m, i), (_, j) in zip(order, turned)]
 
     barrier = pltpu.get_barrier_semaphore()
     for d in LINE:
@@ -350,7 +352,7 @@
         return pl.ds(pl.multiple_of(c * F, F), F)
 
     def seat(i):
-        return pl.ds(i * BLOCK_SLOTS, BLOCK_SLOTS)
+        return pl.ds(pl.multiple_of(i * BLOCK_SLOTS, 16), BLOCK_SLOTS)
 
     def w_copies(k):
         s = k % W_SLOTS
@@ -405,7 +407,7 @@
 
         @pl.when(jnp.logical_not(shared(c)))
         def _():
-            for m, i in order:
+            for m, i in by_core:
                 act_on(seat_copy(c, m, i, *args))
 
     def start(copy):
@@ -617,7 +619,7 @@
 
             @pl.when(jnp.logical_not(shared(c)))
             def _():
-                for m, i in order:
+                for m, i in by_core:
                     seat_copy(c, m, i, back, r_s, r_r, -1).start()
                 back[c, 0, seat(0)] = send[c, 0, seat(0)]
 

time: 235 us -> 236 us (level)
  no operation moved by 1% of the time
where the time goes in v6:
time: 236 us; the launch traced here: 235 us
  Pallas kernels  233 us (99%)
    pallas_call x1, Pallas kernels, experts(): pl.pallas_call(functools.partial(expert_kernel, chunks), out_shape=jax.Sh...  144 us
    pallas_call x1, Pallas kernels, attention(): pl.pallas_call(functools.partial(attention_kernel, chunks), out_shape=[ja...  89.1 us

profile of v6, /device:TPU:1, one launch (start us, length us, event | category | flops | bytes accessed | tf_op | source)
XLA Modules:
  0.0 235.3 jit_solution(4439046886076300828)
XLA Ops:
  0.0 89.1 %attention.1 = (bf16[128,4096]{1,0:T(8,128)(2,1)}, f32[128,4096]{1,0:T(8,128)}, f32[4,8,128]{2,1,0:T(8,128)}, bf16[4096,512]{1,0:T(8,128)(2,1)}, bf16[4096,512]{1,0:T(8,128)(2,1)}, /*index=5*/bf16[512,4096]{1,0:T(8,128)(2,1)}) custom-call(bf16[3,128,4096]{2,1,0:T(8,128)(2,1)} %bitcast.24, bf16[128,4096]{1,0:T(8,128)(2,1)} %bitcast.25, ...), custom_call_target="tpu_custom_call" | custom-call | flops 6499999744 | bytes 40000000 | tf_op jit(solution)/shard_map/attention/pallas_call | solution.py:264
  89.1 143.9 %experts.1 = bf16[128,4096]{1,0:T(8,128)(2,1)} custom-call(bf16[128,4096]{1,0:T(8,128)(2,1)} %get-tuple-element.11.moe_ref, f32[128,4096]{1,0:T(8,128)} %get-tuple-element.12.res_hbm, f32[4,4096]{1,0:T(4,128)} %mod_ref.3, f32[4,8,128]{2,1,0:T(8,128)} %get-tuple-element.13.packs_ref, bf16[4096,512]{1,0:T(8,128)(2,1)} %bitcast.19, ...), custom_call_target="tpu_custom_call" | custom-call | flops 25999998976 | bytes 40000000 | tf_op jit(solution)/shard_map/experts/pallas_call | solution.py:706
  233.0 2.3 copy.12
